TPU v7x, 128 devices: a whole 4x4x4 slice. The times are simulated.
128 devices in a mesh: req: 16 (over y, x), kvh: 8 (over z, core).
Axes of the slice: x: 4, y: 4, z: 4, core: 2. Of those that a mesh axis runs over, the one named last changes fastest.
Arguments:
- queries: bfloat16 [256, 8192], P('req', 'kvh'), may hold values from -150 to 150
- corpus_keys: bfloat16 [65536, 1024], P('req', 'kvh'), may hold values from -6 to 6
- corpus_values: bfloat16 [65536, 1024], P('req', 'kvh'), may hold values from -6 to 6
- task_keys: bfloat16 [32768, 1024], P('req', 'kvh'), may hold values from -7 to 7
- task_values: bfloat16 [32768, 1024], P('req', 'kvh'), may hold values from -6 to 6
- history_keys: bfloat16 [131072, 1024], P('req', 'kvh'), may hold values from -8 to 8
- history_values: bfloat16 [131072, 1024], P('req', 'kvh'), may hold values from -6 to 6
- history_lengths: int32 [256], P('req'), may hold values from 1 to 512, as said below
- task_of: int32 [256], replicated, may hold values from 0 to 7
- out_weight: bfloat16 [8192, 8192], P('kvh'), may hold values from -0.0625 to 0.0625
Outputs:
- mixed: bfloat16 [256, 8192], P('req', 'kvh')
Inputs may be any that keep to these rules, and one draw needn't show every extreme that they name: `history_lengths`: each request's live history rows are its first rows; some request has 512 of them in every draw.
All inputs are finite; a program needn't handle non-finite values.
Results may differ from a plain program's by a relative error of at most 0.014.
Values may be sent and summed in bfloat16 or wider, within the bound.
A program may use at most 128 MiB of HBM per device.

v0:
```python
import math

import jax
import jax.numpy as jnp
from jax import lax
from jax.sharding import PartitionSpec as P

HD = 128
HOLDERS = 2


def in_order(blocks, dim):
    lengths = list(blocks.shape[1:])
    lengths[dim] *= blocks.shape[0]
    return jnp.moveaxis(blocks, 0, dim).reshape(lengths)


def from_everyone(value, axis):
    copies = jnp.broadcast_to(value, (lax.axis_size(axis), *value.shape))
    return lax.all_to_all(copies, axis, split_axis=0, concat_axis=0, tiled=True)


def gathered_copies(value, axis, dim):
    return in_order(from_everyone(value, axis), dim)


def of_everyone(value, axis):
    everything = from_everyone(value, axis)
    return jnp.max(everything, axis=0)


def cut_along(value, dim, size):
    lengths = value.shape
    blocks = value.reshape(*lengths[:dim], size, lengths[dim] // size, *lengths[dim + 1 :])
    return jnp.moveaxis(blocks, dim, 0)


def sum_at_owner(value, axis, dim):
    blocks = cut_along(value, dim, lax.axis_size(axis))
    arrived = lax.all_to_all(blocks, axis, split_axis=0, concat_axis=0, tiled=True)
    return arrived.sum(axis=0)


def side_by_side(arrays, axis, dim, along):
    columns = [a.reshape(*a.shape[:along], -1) for a in arrays]
    both = jnp.concatenate(columns, axis=along)
    out, at, gathered = (sum_at_owner(both, axis, dim), 0, [])
    for a, column in zip(arrays, columns):
        section = out[..., at : at + column.shape[along]]
        gathered.append(section.reshape(*section.shape[:along], *a.shape[along:]))
        at += column.shape[along]
    return tuple(gathered)


def shards(
    queries,
    corpus_keys,
    corpus_values,
    task_keys,
    task_values,
    history_keys,
    history_values,
    history_lengths,
    task_of,
    out_weight,
):
    home_rows = queries.shape[0]
    local_heads = queries.shape[1] // HD
    local_kv = corpus_keys.shape[1] // HD
    group = local_heads // local_kv
    scale = 1.0 / math.sqrt(HD)
    corpus_rows = corpus_keys.shape[0]
    every_query = gathered_copies(queries, "req", 0)
    all_rows = every_query.shape[0]
    block_rows = math.gcd(all_rows, max(1, 512 // local_heads))
    blocks = all_rows // block_rows
    my_task = lax.axis_index("req") // HOLDERS
    keys_here = jnp.concatenate([corpus_keys, task_keys], 0).reshape(-1, local_kv, HD)
    values_here = jnp.concatenate([corpus_values, task_values], 0).reshape(-1, local_kv, HD)
    column = jnp.arange(keys_here.shape[0], dtype=jnp.int32)
    query_blocks = every_query.reshape(blocks, block_rows, local_kv, group, HD)
    task_blocks = task_of.reshape(blocks, block_rows)

    def prefix_block(pieces):
        query_block, task_block = pieces
        scores = (
            jnp.einsum("rkgd,skd->rkgs", query_block, keys_here, preferred_element_type=jnp.float32)
            * scale
        )
        valid = (column[None, :] < corpus_rows) | (task_block[:, None] == my_task)
        valid = valid[:, None, None, :]
        peak_local = jnp.max(jnp.where(valid, scores, -jnp.inf), -1)
        weights = jnp.where(valid, jnp.exp(scores - peak_local[..., None]), 0.0)
        total = jnp.sum(weights, -1)
        summed = jnp.einsum(
            "rkgs,skd->rkgd",
            weights.astype(jnp.bfloat16),
            values_here,
            preferred_element_type=jnp.float32,
        )
        return (summed, peak_local, total)

    summed, peak_local, total = lax.map(prefix_block, (query_blocks, task_blocks))
    summed = summed.reshape(all_rows, local_kv, group, HD)
    peak_local = peak_local.reshape(all_rows, local_kv, group)
    total = total.reshape(all_rows, local_kv, group)
    peak_all = of_everyone(peak_local, "req")
    factor = jnp.exp(peak_local - peak_all)
    prefix_sum, prefix_total = side_by_side(
        (summed * factor[..., None], total * factor), "req", 0, 3
    )
    prefix_peak = lax.dynamic_slice_in_dim(
        peak_all, lax.axis_index("req") * home_rows, home_rows, 0
    )
    own_query = queries.reshape(home_rows, local_kv, group, HD)
    hkeys = history_keys.reshape(home_rows, -1, local_kv, HD)
    hvals = history_values.reshape(home_rows, -1, local_kv, HD)
    hscores = (
        jnp.einsum("rkgd,rtkd->rkgt", own_query, hkeys, preferred_element_type=jnp.float32) * scale
    )
    live = jnp.arange(hkeys.shape[1], dtype=jnp.int32)[None, :] < history_lengths[:, None]
    live = live[:, None, None, :]
    hpeak = jnp.max(jnp.where(live, hscores, -jnp.inf), -1)
    hweights = jnp.where(live, jnp.exp(hscores - hpeak[..., None]), 0.0)
    htotal = jnp.sum(hweights, -1)
    hsum = jnp.einsum(
        "rkgt,rtkd->rkgd", hweights.astype(jnp.bfloat16), hvals, preferred_element_type=jnp.float32
    )
    highest = jnp.maximum(prefix_peak, hpeak)
    prefix_factor = jnp.exp(prefix_peak - highest)
    history_factor = jnp.exp(hpeak - highest)
    numerator = prefix_sum * prefix_factor[..., None] + hsum * history_factor[..., None]
    denominator = prefix_total * prefix_factor + htotal * history_factor
    attended = (
        (numerator / denominator[..., None])
        .reshape(home_rows, local_heads * HD)
        .astype(jnp.bfloat16)
    )
    projected = jnp.dot(attended, out_weight, preferred_element_type=jnp.float32)
    return sum_at_owner(projected, "kvh", 1).astype(jnp.bfloat16)


def solution(mesh):
    return jax.shard_map(
        shards,
        mesh=mesh,
        in_specs=(
            P("req", "kvh"),
            P("req", "kvh"),
            P("req", "kvh"),
            P("req", "kvh"),
            P("req", "kvh"),
            P("req", "kvh"),
            P("req", "kvh"),
            P("req"),
            P(),
            P("kvh", None),
        ),
        out_specs=P("req", "kvh"),
        check_vma=False,
    )
```

profile of v0, /device:TPU:1, one launch (start us, length us, event | category | flops | bytes accessed | tf_op | source)
XLA Modules:
  0.0 157.7 jit_solution(8372911893022903822)
XLA Ops:
  0.0 0.0 copy-start
  0.0 1.8 %broadcast_in_dim.69 = bf16[16,16,1024]{2,1,0:T(8,128)(2,1)} broadcast(bf16[16,1024]{1,0:T(8,128)(2,1)} %param.12), dimensions={1,2} | broadcast | bytes 557056 | tf_op jit(solution)/shard_map/broadcast_in_dim | solution.py:19
  1.8 7.6 %all-to-all-start = ((bf16[16,16,1024]{2,1,0:T(8,128)(2,1)}), bf16[16,16,1024]{2,1,0:T(8,128)(2,1)S(1)}, u32[]{:S(2)}, u32[]{:S(2)}) async-start(bf16[16,16,1024]{2,1,0:T(8,128)(2,1)} %broadcast_in_dim.69), calls=%async_computation | async-start | bytes 1048576 | tf_op jit(solution)/shard_map/all_to_all | solution.py:20
  9.4 0.8 reshape.244
  10.2 3.7 %maximum_bitcast_fusion = (bf16[6144,1,128]{2,0,1:T(8,128)(2,1)}, bf16[6144,1,128]{2,0,1:T(8,128)(2,1)}) fusion(bf16[2048,128]{1,0:T(8,128)(2,1)} %param.15, bf16[4096,128]{1,0:T(8,128)(2,1)} %param.13, bf16[2048,128]{1,0:T(8,128)(2,1)} %param.16, bf16[4096,128]{1,0:T(8,128)(2,1)} %param.14), kind=kLoop, calls=%fused_computation.28 | loop fusion | flops 6291456 | bytes 6291456 | tf_op jit(solution)/shard_map/reshape | solution.py:78
  13.9 6.0 %all-to-all-done = bf16[16,16,1024]{2,1,0:T(8,128)(2,1)S(1)} async-done(((bf16[16,16,1024]{2,1,0:T(8,128)(2,1)}), bf16[16,16,1024]{2,1,0:T(8,128)(2,1)S(1)}, u32[]{:S(2)}, u32[]{:S(2)}) %all-to-all-start) | async-done | bytes 524320 | tf_op jit(solution)/shard_map/all_to_all | solution.py:20
  19.9 0.1 copy.59
  20.0 56.7 %while.15 = (s32[]{:T(128)}, f32[4,64,1,8,128]{4,3,1,2,0:T(8,128)}, f32[4,64,1,8]{3,1,2,0:T(8,128)}, f32[4,64,1,8]{3,1,2,0:T(8,128)}, s32[4,64]{1,0:T(4,128)S(1)...) while((s32[]{:T(128)}, f32[4,64,1,8,128]{4,3,1,2,0:T(8,128)}, ...), condition=%wide.region_3.4_spmd.clone, body=%wide.region_0.3_spmd.clone.sunk | while | flops 1645614080 | bytes 42952176 | solution.py:103
  20.0 0.2 broadcast_or_fusion.2
  20.3 4.4 %fusion.57 = (f32[64,8]{1,0:T(8,128)S(1)}, f32[64,8,6144]{2,1,0:T(8,128)S(1)}) fusion(pred[64,6144]{1,0:T(8,128)(4,1)S(1)} %broadcast_or_fusion.2, bf16[6144,1,128]{2,0,1:T(8,128)(2,1)} %get-tuple-element.219, bf16[4,64,1,8,128]{4,3,1,2,0:T(8,128)(2,1)S(1)} %get-tuple-element.218, s32[]{:T(128)} %get-tuple-element.202), kind=kOutput, calls=%fused_computation.3.clone.1 | convolution fusion | flops 814743040 | bytes 14682116 | tf_op jit(solution)/shard_map/while/body/eval_jaxpr/rkgd,skd->rkgs/dot_general | solution.py:87
  24.7 3.8 %fusion.59 = f32[64,8]{1,0:T(8,128)S(1)} fusion(f32[64,8,6144]{2,1,0:T(8,128)S(1)} %get-tuple-element.188, f32[64,8]{1,0:T(8,128)S(1)} %get-tuple-element.189, pred[64,6144]{1,0:T(8,128)(4,1)S(1)} %broadcast_or_fusion.2), kind=kLoop, calls=%fused_computation.6.clone.1 | loop fusion | flops 12582400 | bytes 12980224 | tf_op jit(solution)/shard_map/while/body/eval_jaxpr/reduce_sum | solution.py:94
  28.5 0.6 bitcast_dynamic-update-slice_fusion.3
  29.2 5.0 %fusion.58 = f32[4,64,1,8,128]{4,3,1,2,0:T(8,128)} fusion(f32[4,64,1,8,128]{4,3,1,2,0:T(8,128)} %get-tuple-element.203, s32[]{:T(128)} %get-tuple-element.202, bf16[6144,1,128]{2,0,1:T(8,128)(2,1)} %get-tuple-element.220, f32[64,8,6144]{2,1,0:T(8,128)S(1)} %get-tuple-element.188, f32[64,8]{1,0:T(8,128)S(1)} %get-tuple-element.189, ...), kind=kOutput, calls=%fused_computation.15.clone.1 | convolution fusion | flops 817889280 | bytes 14813696 | tf_op jit(solution)/shard_map/while/body/eval_jaxpr/rkgs,skd->rkgd/dot_general | solution.py:95
  34.2 0.2 broadcast_or_fusion.2
  34.4 4.4 %fusion.57 = (f32[64,8]{1,0:T(8,128)S(1)}, f32[64,8,6144]{2,1,0:T(8,128)S(1)}) fusion(pred[64,6144]{1,0:T(8,128)(4,1)S(1)} %broadcast_or_fusion.2, bf16[6144,1,128]{2,0,1:T(8,128)(2,1)} %get-tuple-element.219, bf16[4,64,1,8,128]{4,3,1,2,0:T(8,128)(2,1)S(1)} %get-tuple-element.218, s32[]{:T(128)} %get-tuple-element.202), kind=kOutput, calls=%fused_computation.3.clone.1 | convolution fusion | flops 814743040 | bytes 14682116 | tf_op jit(solution)/shard_map/while/body/eval_jaxpr/rkgd,skd->rkgs/dot_general | solution.py:87
  38.9 3.8 %fusion.59 = f32[64,8]{1,0:T(8,128)S(1)} fusion(f32[64,8,6144]{2,1,0:T(8,128)S(1)} %get-tuple-element.188, f32[64,8]{1,0:T(8,128)S(1)} %get-tuple-element.189, pred[64,6144]{1,0:T(8,128)(4,1)S(1)} %broadcast_or_fusion.2), kind=kLoop, calls=%fused_computation.6.clone.1 | loop fusion | flops 12582400 | bytes 12980224 | tf_op jit(solution)/shard_map/while/body/eval_jaxpr/reduce_sum | solution.py:94
  42.7 0.6 bitcast_dynamic-update-slice_fusion.3
  43.4 5.0 %fusion.58 = f32[4,64,1,8,128]{4,3,1,2,0:T(8,128)} fusion(f32[4,64,1,8,128]{4,3,1,2,0:T(8,128)} %get-tuple-element.203, s32[]{:T(128)} %get-tuple-element.202, bf16[6144,1,128]{2,0,1:T(8,128)(2,1)} %get-tuple-element.220, f32[64,8,6144]{2,1,0:T(8,128)S(1)} %get-tuple-element.188, f32[64,8]{1,0:T(8,128)S(1)} %get-tuple-element.189, ...), kind=kOutput, calls=%fused_computation.15.clone.1 | convolution fusion | flops 817889280 | bytes 14813696 | tf_op jit(solution)/shard_map/while/body/eval_jaxpr/rkgs,skd->rkgd/dot_general | solution.py:95
  48.4 0.2 broadcast_or_fusion.2
  48.6 4.4 %fusion.57 = (f32[64,8]{1,0:T(8,128)S(1)}, f32[64,8,6144]{2,1,0:T(8,128)S(1)}) fusion(pred[64,6144]{1,0:T(8,128)(4,1)S(1)} %broadcast_or_fusion.2, bf16[6144,1,128]{2,0,1:T(8,128)(2,1)} %get-tuple-element.219, bf16[4,64,1,8,128]{4,3,1,2,0:T(8,128)(2,1)S(1)} %get-tuple-element.218, s32[]{:T(128)} %get-tuple-element.202), kind=kOutput, calls=%fused_computation.3.clone.1 | convolution fusion | flops 814743040 | bytes 14682116 | tf_op jit(solution)/shard_map/while/body/eval_jaxpr/rkgd,skd->rkgs/dot_general | solution.py:87
  53.1 3.8 %fusion.59 = f32[64,8]{1,0:T(8,128)S(1)} fusion(f32[64,8,6144]{2,1,0:T(8,128)S(1)} %get-tuple-element.188, f32[64,8]{1,0:T(8,128)S(1)} %get-tuple-element.189, pred[64,6144]{1,0:T(8,128)(4,1)S(1)} %broadcast_or_fusion.2), kind=kLoop, calls=%fused_computation.6.clone.1 | loop fusion | flops 12582400 | bytes 12980224 | tf_op jit(solution)/shard_map/while/body/eval_jaxpr/reduce_sum | solution.py:94
  56.9 0.6 bitcast_dynamic-update-slice_fusion.3
  57.5 5.0 %fusion.58 = f32[4,64,1,8,128]{4,3,1,2,0:T(8,128)} fusion(f32[4,64,1,8,128]{4,3,1,2,0:T(8,128)} %get-tuple-element.203, s32[]{:T(128)} %get-tuple-element.202, bf16[6144,1,128]{2,0,1:T(8,128)(2,1)} %get-tuple-element.220, f32[64,8,6144]{2,1,0:T(8,128)S(1)} %get-tuple-element.188, f32[64,8]{1,0:T(8,128)S(1)} %get-tuple-element.189, ...), kind=kOutput, calls=%fused_computation.15.clone.1 | convolution fusion | flops 817889280 | bytes 14813696 | tf_op jit(solution)/shard_map/while/body/eval_jaxpr/rkgs,skd->rkgd/dot_general | solution.py:95
  62.5 0.2 broadcast_or_fusion.2
  62.8 4.4 %fusion.57 = (f32[64,8]{1,0:T(8,128)S(1)}, f32[64,8,6144]{2,1,0:T(8,128)S(1)}) fusion(pred[64,6144]{1,0:T(8,128)(4,1)S(1)} %broadcast_or_fusion.2, bf16[6144,1,128]{2,0,1:T(8,128)(2,1)} %get-tuple-element.219, bf16[4,64,1,8,128]{4,3,1,2,0:T(8,128)(2,1)S(1)} %get-tuple-element.218, s32[]{:T(128)} %get-tuple-element.202), kind=kOutput, calls=%fused_computation.3.clone.1 | convolution fusion | flops 814743040 | bytes 14682116 | tf_op jit(solution)/shard_map/while/body/eval_jaxpr/rkgd,skd->rkgs/dot_general | solution.py:87
  67.2 3.8 %fusion.59 = f32[64,8]{1,0:T(8,128)S(1)} fusion(f32[64,8,6144]{2,1,0:T(8,128)S(1)} %get-tuple-element.188, f32[64,8]{1,0:T(8,128)S(1)} %get-tuple-element.189, pred[64,6144]{1,0:T(8,128)(4,1)S(1)} %broadcast_or_fusion.2), kind=kLoop, calls=%fused_computation.6.clone.1 | loop fusion | flops 12582400 | bytes 12980224 | tf_op jit(solution)/shard_map/while/body/eval_jaxpr/reduce_sum | solution.py:94
  71.1 0.6 bitcast_dynamic-update-slice_fusion.3
  71.7 5.0 %fusion.58 = f32[4,64,1,8,128]{4,3,1,2,0:T(8,128)} fusion(f32[4,64,1,8,128]{4,3,1,2,0:T(8,128)} %get-tuple-element.203, s32[]{:T(128)} %get-tuple-element.202, bf16[6144,1,128]{2,0,1:T(8,128)(2,1)} %get-tuple-element.220, f32[64,8,6144]{2,1,0:T(8,128)S(1)} %get-tuple-element.188, f32[64,8]{1,0:T(8,128)S(1)} %get-tuple-element.189, ...), kind=kOutput, calls=%fused_computation.15.clone.1 | convolution fusion | flops 817889280 | bytes 14813696 | tf_op jit(solution)/shard_map/while/body/eval_jaxpr/rkgs,skd->rkgd/dot_general | solution.py:95
  76.7 1.0 copy.42
  77.7 0.7 broadcast_in_dim.70
  78.3 3.5 %all-to-all-start.1 = ((f32[16,256,1,8]{1,3,2,0:T(8,128)}), f32[16,256,1,8]{1,3,2,0:T(8,128)S(1)}, u32[]{:S(2)}, u32[]{:S(2)}) async-start(f32[16,256,1,8]{1,3,2,0:T(8,128)} %broadcast_in_dim.70), calls=%async_computation.1 | async-start | bytes 262144 | tf_op jit(solution)/shard_map/all_to_all | solution.py:20
  81.9 1.0 copy.43
  82.9 1.0 copy.56
  83.9 1.0 copy.57
  84.9 3.8 %all-to-all-done.1 = f32[16,256,1,8]{1,3,2,0:T(8,128)S(1)} async-done(((f32[16,256,1,8]{1,3,2,0:T(8,128)}), f32[16,256,1,8]{1,3,2,0:T(8,128)S(1)}, u32[]{:S(2)}, u32[]{:S(2)}) %all-to-all-start.1) | async-done | bytes 131104 | tf_op jit(solution)/shard_map/all_to_all | solution.py:20
  88.7 0.1 reduce_max.32
  88.8 0.1 reduce_max.33
  88.9 0.1 copy.44
  89.0 0.8 copy.47
  89.8 1.6 broadcast_multiply_fusion
  91.4 1.5 pad_maximum_fusion
  92.9 0.0 copy-start.1
  92.9 0.0 copy-start.2
  92.9 4.7 %all-to-all-start.2 = ((f32[16,16,1,8,129]{4,3,1,2,0:T(8,128)}), f32[16,16,1,8,129]{4,3,1,2,0:T(8,128)}, u32[]{:S(2)}, u32[]{:S(2)}) async-start(f32[16,16,1,8,129]{4,3,1,2,0:T(8,128)} %pad_maximum_fusion), calls=%async_computation.2 | async-start | bytes 4194304 | tf_op jit(solution)/shard_map/all_to_all | solution.py:40
  97.6 0.0 copy-done.1
  97.7 0.0 copy-done.2
  97.7 0.1 iota_compare_fusion.1
  97.7 0.0 copy-done
  97.7 0.7 select_reduce_fusion
  98.5 0.1 copy.48
  98.5 0.2 fusion.33
  98.8 0.1 copy.53
  98.8 22.4 %copy.58 = bf16[8192,1024]{1,0:T(8,128)(2,1)} copy(bf16[8192,1024]{0,1:T(8,128)(2,1)} %bitcast.136) | data formatting | bytes 33554432 | tf_op jit(solution)/shard_map/dot_general | solution.py:139
  121.3 1.2 all-to-all-done.2
  122.5 1.7 %reduce_sum.38 = f32[16,8,129]{2,1,0:T(8,128)S(1)} reduce(f32[16,16,1,8,129]{4,3,1,2,0:T(8,128)} %all-to-all-done.2, f32[]{:T(128)} %constant.46.clone.1), dimensions={0,2}, to_apply=%region_5.6 | reduce | flops 247680 | bytes 1122820 | tf_op jit(solution)/shard_map/reduce_sum | solution.py:41
  124.3 0.1 copy.52
  124.4 0.1 fusion.41
  124.5 0.1 copy.49
  124.5 0.1 copy.51
  124.6 0.1 copy.54
  124.7 2.0 %fusion.32 = bf16[16,1,8,128]{3,2,0,1:T(8,128)(2,1)S(1)} fusion(bf16[16,512,128]{2,1,0:T(8,128)(2,1)} %bitcast.138, f32[16,8,512]{2,1,0:T(8,128)S(1)} %get-tuple-element.126, f32[16,8]{1,0:T(8,128)S(1)} %get-tuple-element.125, pred[16,512]{1,0:T(8,128)(4,1)S(1)} %iota_compare_fusion.1, f32[16,1,8,129]{3,2,0,1:T(8,128)S(1)} %bitcast.145, ...), kind=kOutput, calls=%fused_computation.36 | convolution fusion | flops 17055744 | bytes 2467840 | tf_op jit(solution)/shard_map/rkgt,rtkd->rkgd/dot_general | solution.py:126
  126.8 10.2 %convolution_bitcast_fusion = f32[8,16,1024]{2,1,0:T(8,128)S(1)} fusion(bf16[16,1024,1]{1,0,2:T(8,128)(2,1)S(1)} %reshape.262, bf16[8,1024,1024]{2,1,0:T(8,128)(2,1)} %bitcast.135), kind=kOutput, calls=%fused_computation.30 | convolution fusion | flops 268435456 | bytes 17334272 | tf_op jit(solution)/shard_map/dot_general | solution.py:139
  137.0 20.1 %all_to_all.20 = f32[8,16,1024]{2,1,0:T(8,128)S(1)} all-to-all(f32[8,16,1024]{2,1,0:T(8,128)S(1)} %convolution_bitcast_fusion), channel_id=1, replica_groups=mesh['req'=16,'kvh'=8] {'kvh'}, dimensions={0} | all-to-all | bytes 1048576 | tf_op jit(solution)/shard_map/all_to_all | solution.py:40
  157.1 0.6 reduce_sum.41
  (17 shorter events, 0.2 us)
Async XLA Ops:
  0.0 97.7 %copy-start = (bf16[8192,128]{1,0:T(8,128)(2,1)S(1)}, bf16[8192,128]{1,0:T(8,128)(2,1)}, u32[]{:S(2)}) copy-start(bf16[8192,128]{1,0:T(8,128)(2,1)} %param.17) | copy-start | bytes 6291460
  1.8 18.1 %all-to-all-start = ((bf16[16,16,1024]{2,1,0:T(8,128)(2,1)}), bf16[16,16,1024]{2,1,0:T(8,128)(2,1)S(1)}, u32[]{:S(2)}, u32[]{:S(2)}) async-start(bf16[16,16,1024]{2,1,0:T(8,128)(2,1)} %broadcast_in_dim.69), calls=%async_computation | async-start | bytes 1048576 | tf_op jit(solution)/shard_map/all_to_all | solution.py:20
  78.3 10.3 %all-to-all-start.1 = ((f32[16,256,1,8]{1,3,2,0:T(8,128)}), f32[16,256,1,8]{1,3,2,0:T(8,128)S(1)}, u32[]{:S(2)}, u32[]{:S(2)}) async-start(f32[16,256,1,8]{1,3,2,0:T(8,128)} %broadcast_in_dim.70), calls=%async_computation.1 | async-start | bytes 262144 | tf_op jit(solution)/shard_map/all_to_all | solution.py:20
  92.9 4.8 %copy-start.1 = (bf16[16,1024]{1,0:T(8,128)(2,1)S(1)}, bf16[16,1024]{1,0:T(8,128)(2,1)}, u32[]{:S(2)}) copy-start(bf16[16,1024]{1,0:T(8,128)(2,1)} %param.12) | copy-start | bytes 98308
  92.9 4.8 %copy-start.2 = (s32[16]{0:T(128)S(1)}, s32[16]{0:T(128)}, u32[]{:S(2)}) copy-start(s32[16]{0:T(128)} %param.19) | copy-start | bytes 196
  92.9 29.6 %all-to-all-start.2 = ((f32[16,16,1,8,129]{4,3,1,2,0:T(8,128)}), f32[16,16,1,8,129]{4,3,1,2,0:T(8,128)}, u32[]{:S(2)}, u32[]{:S(2)}) async-start(f32[16,16,1,8,129]{4,3,1,2,0:T(8,128)} %pad_maximum_fusion), calls=%async_computation.2 | async-start | bytes 4194304 | tf_op jit(solution)/shard_map/all_to_all | solution.py:40
where the time goes:
time: 159 us; the launch traced here: 158 us
  matrix products  50.8 us (32%)
  local copies, waits for them, and re-layouts  33.8 us (21%)
  other arithmetic  25.9 us (16%)
  blocking collectives  20.1 us (13%)
  starting transfers between devices  15.8 us (10%)
  waiting for transfers between devices  11 us (7%)
    dot_general x1, local copies, waits for them, and re-layouts, shards(): jnp.dot(attended, out_weight, preferred_element_type=jnp.float32)  22.4 us
    all_to_all x1, blocking collectives, sum_at_owner(): lax.all_to_all(blocks, axis, split_axis=0, concat_axis=0, tiled=True)  20.1 us
    dot_general x4, matrix products, prefix_block(): jnp.einsum('rkgs,skd->rkgd', weights.astype(jnp.bfloat16), values_here, p...  20 us
    dot_general x4, matrix products, prefix_block(): jnp.einsum('rkgd,skd->rkgs', query_block, keys_here, preferred_element_ty...  17.8 us
    reduce_sum x4, other arithmetic, prefix_block(): total = jnp.sum(weights, -1)  15.3 us
    all_to_all x2, starting transfers between devices, from_everyone(): return lax.all_to_all(copies, axis, split_axis=0, concat_axis=0, tiled=True)  11.1 us
    dot_general x1, matrix products, shards(): jnp.dot(attended, out_weight, preferred_element_type=jnp.float32)  10.2 us
    all_to_all x2, waiting for transfers between devices, from_everyone(): return lax.all_to_all(copies, axis, split_axis=0, concat_axis=0, tiled=True)  9.75 us
  transfers between devices with their start and end apart: 3, of which 3 were waited for; matrix products, arithmetic and copies ran while one was open for 20% of the time, Pallas kernels for 0%

commit v1 on v0

v1 whole, which is shorter than its diff:
```python
import functools
import math

import jax
import jax.numpy as jnp
from jax import lax
from jax.experimental import pallas as pl
from jax.experimental.pallas import tpu as pltpu
from jax.sharding import PartitionSpec as P

HD = 128
HOLDERS = 2
MESH = pl.DeviceIdType.MESH
F32 = jnp.float32
BF16 = jnp.bfloat16
CS = math.log2(math.e) / math.sqrt(HD)
FAR = 1e30
NT = (((1,), (1,)), ((), ()))
TN = (((0,), (0,)), ((), ()))


def ring4(a):
    return a + a // 2 - 2 * (a // 3)


def kernel(
    q_hbm,
    ck_hbm,
    cv_hbm,
    tk_hbm,
    tv_hbm,
    hk_hbm,
    hv_hbm,
    len_ref,
    task_ref,
    w_hbm,
    out_ref,
    q_all,
    kbuf,
    vbuf,
    vt,
    hkb,
    hvb,
    wbuf,
    sa,
    sb,
    osend,
    orecv,
    hs,
    hq,
    hot,
    hlse,
    valid,
    psend,
    precv,
    ld_sem,
    q_send,
    q_recv,
    o_send,
    o_recv,
    p_send,
    p_recv,
):
    nreq, rows, width = q_all.shape
    nkv = psend.shape[0]
    heads = width // HD
    cols = rows * heads
    corpus = ck_hbm.shape[0]
    keys = kbuf.shape[0]
    hist = hkb.shape[0] // rows
    out_w = psend.shape[2]
    chunk = 512
    nch, ncorp = keys // chunk, corpus // chunk
    me = lax.axis_index("req")
    mj = lax.axis_index("kvh")
    y, x = me // 4, me % 4
    mz, mc = mj // 2, mj % 2

    def peer(k, sign):
        dy, dx = ring4(k // 4), ring4(k % 4)
        return ((y + 4 + sign * dy) % 4) * 4 + (x + 4 + sign * dx) % 4

    def kv_peer(e, sign):
        dz, dc = ring4(e // 2), e % 2
        return ((mz + 4 + sign * dz) % 4) * 2 + (mc + dc) % 2

    loads = [
        pltpu.make_async_copy(q_hbm, q_all.at[0], ld_sem.at[0]),
        pltpu.make_async_copy(hk_hbm, hkb, ld_sem.at[1]),
        pltpu.make_async_copy(hv_hbm, hvb, ld_sem.at[2]),
        pltpu.make_async_copy(cv_hbm, vbuf.at[pl.ds(0, corpus)], ld_sem.at[3]),
        pltpu.make_async_copy(tv_hbm, vbuf.at[pl.ds(corpus, keys - corpus)], ld_sem.at[4]),
        pltpu.make_async_copy(ck_hbm, kbuf.at[pl.ds(0, corpus)], ld_sem.at[5]),
        pltpu.make_async_copy(tk_hbm, kbuf.at[pl.ds(corpus, keys - corpus)], ld_sem.at[6]),
        pltpu.make_async_copy(w_hbm, wbuf, ld_sem.at[7]),
    ]
    for c in loads:
        c.start()

    barrier = pltpu.get_barrier_semaphore()

    def greet_req(k, carry):
        pl.semaphore_signal(barrier, inc=1, device_id={"req": peer(k, 1)}, device_id_type=MESH)
        return carry

    def greet_kv(e, carry):
        pl.semaphore_signal(barrier, inc=1, device_id={"kvh": kv_peer(e, 1)}, device_id_type=MESH)
        return carry

    lax.fori_loop(1, nreq, greet_req, 0)
    lax.fori_loop(1, nkv, greet_kv, 0)
    pl.semaphore_wait(barrier, nreq + nkv - 2)

    loads[0].wait()

    def q_copy(k):
        return pltpu.make_async_remote_copy(
            src_ref=q_all.at[0],
            dst_ref=q_all.at[k],
            send_sem=q_send.at[k],
            recv_sem=q_recv.at[k],
            device_id={"req": peer(k, -1)},
            device_id_type=MESH,
        )

    def send_q(k, carry):
        q_copy(k).start()
        return carry

    lax.fori_loop(1, nreq, send_q, 0)

    def head_major(k):
        block = q_all[k]
        return [block[:, h * HD : (h + 1) * HD] for h in range(heads)]

    lane = lax.broadcasted_iota(jnp.int32, (nreq, nreq * rows), 1)
    row = lax.broadcasted_iota(jnp.int32, (nreq, nreq * rows), 0)
    mine = jnp.broadcast_to(task_ref[...], lane.shape) == me // HOLDERS
    mine = jnp.where(mine & (lane // rows == row), 1.0, 0.0).astype(BF16)
    er = lax.broadcasted_iota(jnp.int32, (nreq * rows, cols), 0)
    ec = lax.broadcasted_iota(jnp.int32, (nreq * rows, cols), 1)
    spread = jnp.where(er % rows == ec % rows, 1.0, 0.0).astype(BF16)
    valid[...] = jnp.dot(mine, spread, preferred_element_type=F32)

    pr = lax.broadcasted_iota(jnp.int32, (cols, cols), 0)
    pc = lax.broadcasted_iota(jnp.int32, (cols, cols), 1)
    perm = jnp.where((pr % heads == pc // rows) & (pr // heads == pc % rows), 1.0, 0.0)
    perm16 = perm.astype(BF16)
    hq[...] = jnp.dot(perm16, jnp.concatenate(head_major(0), 0), preferred_element_type=F32)
    loads[1].wait()
    hcol = lax.broadcasted_iota(jnp.int32, (heads, hist), 1)
    for r in range(rows):
        at = slice(r * heads, (r + 1) * heads)
        s = lax.dot_general(
            hq[at, :].astype(BF16),
            hkb[r * hist : (r + 1) * hist, :],
            NT,
            preferred_element_type=F32,
        )
        hs[at, :] = jnp.where(hcol < len_ref[r], s, -FAR)
    s = hs[...]
    hm = jnp.max(s, axis=1, keepdims=True)
    p = jnp.exp2((s - hm) * CS)
    htot = jnp.sum(p, axis=1, keepdims=True)
    hs[...] = p
    loads[2].wait()
    for r in range(rows):
        at = slice(r * heads, (r + 1) * heads)
        hq[at, :] = jnp.dot(
            hs[at, :].astype(BF16), hvb[r * hist : (r + 1) * hist, :], preferred_element_type=F32
        )
    ho = (hq[...] * (1.0 / htot)).astype(BF16)
    hot[...] = lax.dot_general(ho, perm16, TN, preferred_element_type=F32)
    hl = jnp.sum(perm * (hm * CS + jnp.log2(htot)), axis=0, keepdims=True)
    hlse[...] = jnp.broadcast_to(hl, hlse.shape)

    loads[3].wait()
    loads[4].wait()
    for c in range(nch):
        at = slice(c * chunk, (c + 1) * chunk)
        vt[:HD, at] = vbuf[at, :].T
    vt[HD:, :] = jnp.ones((vt.shape[0] - HD, keys), BF16)
    loads[5].wait()
    loads[6].wait()

    def arrive(b):
        for a in range(2):
            k = 2 * b + a
            if isinstance(b, int) and k == 0:
                continue
            q_copy(k).wait_recv()

    def q_block(b):
        return jnp.concatenate(head_major(2 * b) + head_major(2 * b + 1), 0)

    def score(c, q, sref, peaks):
        at = slice(c * chunk, (c + 1) * chunk)
        s = lax.dot_general(kbuf[at, :], q, NT, preferred_element_type=F32)
        sref[at, :] = s
        part = jnp.max(s.reshape(chunk // 8, 8, 2 * cols), axis=0)
        g = 0 if c < ncorp else 1
        peaks[g] = part if peaks[g] is None else jnp.maximum(peaks[g], part)

    def weigh(c, sref, shifts, acc):
        at = slice(c * chunk, (c + 1) * chunk)
        p = jnp.exp2(sref[at, :] * CS - shifts[0 if c < ncorp else 1]).astype(BF16)
        part = jnp.dot(vt[:, at], p, preferred_element_type=F32)
        return part if acc is None else acc + part

    def o_copy(k):
        return pltpu.make_async_remote_copy(
            src_ref=osend.at[k],
            dst_ref=orecv.at[k],
            send_sem=o_send.at[k],
            recv_sem=o_recv.at[k],
            device_id={"req": peer(k, 1)},
            device_id_type=MESH,
        )

    def stage(b, s_now, s_next, peaks):
        mask = jnp.concatenate([valid[pl.ds(peer(2 * b + a, 1), 1), :] for a in range(2)], 1) > 0
        pk = [jnp.max(m, axis=0, keepdims=True) for m in peaks]
        top = jnp.maximum(pk[0], jnp.where(mask, pk[1], -FAR)) * CS
        shifts = [top, jnp.where(mask, top, FAR)]
        later = [None, None]
        if s_next is not None:
            arrive(b + 1)
            q = q_block(b + 1)
        acc = None
        for c in range(nch):
            if s_next is not None:
                score(c, q, s_next, later)
            acc = weigh(c, s_now, shifts, acc)
        total = acc[HD : HD + 1, :]
        o = (acc[:HD, :] * (1.0 / total)).astype(BF16)
        lse = top + jnp.log2(total)
        hi = lse.astype(BF16).astype(F32)
        mid = (lse - hi).astype(BF16).astype(F32)
        lo = lse - hi - mid
        sub = lax.broadcasted_iota(jnp.int32, (16, 2 * cols), 0)
        info = jnp.where(sub == 0, hi, jnp.where(sub == 1, mid, jnp.where(sub == 2, lo, 0.0)))
        info = info.astype(BF16)
        for a in range(2):
            k = 2 * b + a
            at = slice(a * cols, (a + 1) * cols)
            osend[k, :HD, :] = o[:, at]
            osend[k, HD:, :] = info[:, at]
            if isinstance(k, int):
                if k > 0:
                    o_copy(k).start()
            else:
                pl.when(k > 0)(lambda k=k: o_copy(k).start())
        return later

    arrive(0)
    peaks = [None, None]
    q0 = q_block(0)
    for c in range(nch):
        score(c, q0, sa, peaks)

    def pair(i, peaks):
        peaks = stage(2 * i, sa, sb, list(peaks))
        peaks = stage(2 * i + 1, sb, sa, peaks)
        return tuple(peaks)

    nb = nreq // 2
    peaks = list(lax.fori_loop(0, nb // 2 - 1, pair, tuple(peaks)))
    peaks = stage(nb - 2, sa, sb, peaks)
    stage(nb - 1, sb, None, peaks)

    def arrived(k, carry):
        o_copy(k).wait_recv()
        return carry

    lax.fori_loop(1, nreq, arrived, 0)

    def part(k):
        return osend if k == 0 else orecv

    lses = [
        jnp.sum(part(k)[k, HD:, :].astype(F32), axis=0, keepdims=True) for k in range(nreq)
    ]
    lses.append(hlse[0:1, :])
    top = functools.reduce(jnp.maximum, lses)
    ws = [jnp.exp2(v - top) for v in lses]
    den = functools.reduce(jnp.add, ws)
    att = hot[...] * ws[nreq]
    for k in range(nreq):
        att = att + part(k)[k, :HD, :].astype(F32) * ws[k]
    att = (att * (1.0 / den)).T.astype(BF16)
    att = jnp.concatenate([att[h * rows : (h + 1) * rows, :] for h in range(heads)], 1)

    loads[7].wait()

    def p_copy(e):
        return pltpu.make_async_remote_copy(
            src_ref=psend.at[e],
            dst_ref=precv.at[e],
            send_sem=p_send.at[e],
            recv_sem=p_recv.at[e],
            device_id={"kvh": kv_peer(e, 1)},
            device_id_type=MESH,
        )

    def project(e):
        at = pl.ds(pl.multiple_of(kv_peer(e, 1) * out_w, out_w), out_w)
        return jnp.dot(att, wbuf[:, at], preferred_element_type=F32)

    def send_p(t, carry):
        e = nkv - 1 - t
        psend[e] = project(e).astype(BF16)
        p_copy(e).start()
        return carry

    lax.fori_loop(0, nkv - 1, send_p, 0)
    mixed = project(0)
    for e in range(1, nkv):
        p_copy(e).wait_recv()
        mixed = mixed + precv[e].astype(F32)
    out_ref[...] = mixed.astype(BF16)

    def sent(k, carry):
        q_copy(k).wait_send()
        o_copy(k).wait_send()
        return carry

    lax.fori_loop(1, nreq, sent, 0)

    def p_sent(e, carry):
        p_copy(e).wait_send()
        return carry

    lax.fori_loop(1, nkv, p_sent, 0)


def solution(mesh):
    nreq, nkv = mesh.shape["req"], mesh.shape["kvh"]

    def shards(q, ck, cv, tk, tv, hk, hv, lengths, task_of, w):
        rows, width = q.shape
        cols = rows * (width // HD)
        keys = ck.shape[0] + tk.shape[0]
        hist = hk.shape[0] // rows
        out_w = w.shape[1] // nkv
        hbm = pl.BlockSpec(memory_space=pl.ANY)
        vmem = pl.BlockSpec(memory_space=pltpu.VMEM)
        smem = pl.BlockSpec(memory_space=pltpu.SMEM)
        dma = pltpu.SemaphoreType.DMA
        return pl.pallas_call(
            kernel,
            out_shape=jax.ShapeDtypeStruct((rows, out_w), BF16),
            in_specs=[hbm] * 7 + [smem, vmem, hbm],
            out_specs=vmem,
            scratch_shapes=[
                pltpu.VMEM((nreq, rows, width), BF16),
                pltpu.VMEM((keys, HD), BF16),
                pltpu.VMEM((keys, HD), BF16),
                pltpu.VMEM((HD + 16, keys), BF16),
                pltpu.VMEM(hk.shape, BF16),
                pltpu.VMEM(hv.shape, BF16),
                pltpu.VMEM(w.shape, BF16),
                pltpu.VMEM((keys, 2 * cols), F32),
                pltpu.VMEM((keys, 2 * cols), F32),
                pltpu.VMEM((nreq, HD + 16, cols), BF16),
                pltpu.VMEM((nreq, HD + 16, cols), BF16),
                pltpu.VMEM((cols, hist), F32),
                pltpu.VMEM((cols, HD), F32),
                pltpu.VMEM((HD, cols), F32),
                pltpu.VMEM((8, cols), F32),
                pltpu.VMEM((nreq, cols), F32),
                pltpu.VMEM((nkv, rows, out_w), BF16),
                pltpu.VMEM((nkv, rows, out_w), BF16),
                dma((8,)),
                dma((nreq,)),
                dma((nreq,)),
                dma((nreq,)),
                dma((nreq,)),
                dma((nkv,)),
                dma((nkv,)),
            ],
            compiler_params=pltpu.CompilerParams(
                collective_id=0, has_side_effects=True, vmem_limit_bytes=60 * 2**20
            ),
        )(q, ck, cv, tk, tv, hk, hv, lengths, task_of.reshape(1, -1), w)

    return jax.shard_map(
        shards,
        mesh=mesh,
        in_specs=(P("req", "kvh"),) * 7 + (P("req"), P(), P("kvh", None)),
        out_specs=P("req", "kvh"),
        check_vma=False,
    )
```

time: 159 us -> 40.9 us (0.26)
  matrix products: 50.8 us -> 0 us
  Pallas kernels: 0 us -> 39.3 us
  local copies, waits for them, and re-layouts: 33.8 us -> 1.38 us
  other arithmetic: 25.9 us -> 0 us
  blocking collectives: 20.1 us -> 0 us
  starting transfers between devices: 15.8 us -> 0 us
  waiting for transfers between devices: 11 us -> 0 us
    dot_general x11 -> x0, matrix products: 50.8 us -> none  [the longest x4 20 us: prefix_block(): jnp.einsum('rkgs,skd->rkgd', weights.astype(jnp.bfloat16), values_here, p...]
    pallas_call x0 -> x1, Pallas kernels: none -> 39.3 us  [shards(): pl.pallas_call(kernel, out_shape=jax.ShapeDtypeStruct((rows, out_w), BF16...]
    dot_general x1 -> x0, local copies, waits for them, and re-layouts: 22.4 us -> none  [shards(): jnp.dot(attended, out_weight, preferred_element_type=jnp.float32)]
    all_to_all x1 -> x0, blocking collectives: 20.1 us -> none  [sum_at_owner(): lax.all_to_all(blocks, axis, split_axis=0, concat_axis=0, tiled=True)]
    reduce_sum x7 -> x0, other arithmetic: 17.9 us -> none  [the longest x4 15.3 us: prefix_block(): total = jnp.sum(weights, -1)]
    all_to_all x3 -> x0, starting transfers between devices: 15.8 us -> none  [the longest x2 11.1 us: from_everyone(): return lax.all_to_all(copies, axis, split_axis=0, concat_axis=0, tiled=True)]
    all_to_all x3 -> x0, waiting for transfers between devices: 11 us -> none  [the longest x2 9.75 us: from_everyone(): return lax.all_to_all(copies, axis, split_axis=0, concat_axis=0, tiled=True)]
    reshape x5 -> x0, local copies, waits for them, and re-layouts: 4.74 us -> none  [the longest x3 2.97 us: shards(): peak_local = peak_local.reshape(all_rows, local_kv, group)]
  transfers between devices with their start and end apart: 3 -> 0, of which waited for: 3 -> 0; matrix products, arithmetic and copies ran while one was open for 20% -> 0% of each run, Pallas kernels for 0% -> 0%
where the time goes in v1:
time: 40.9 us; the launch traced here: 40.7 us
  Pallas kernels  39.3 us (96%)
  local copies, waits for them, and re-layouts  1.38 us (3%)
    pallas_call x1, Pallas kernels, shards(): pl.pallas_call(kernel, out_shape=jax.ShapeDtypeStruct((rows, out_w), BF16...  39.3 us
    unnamed x1, local copies, waits for them, and re-layouts  1.38 us

profile of v1, /device:TPU:1, one launch (start us, length us, event | category | flops | bytes accessed | tf_op | source)
XLA Modules:
  0.0 40.7 jit_solution(15391895133091352546)
XLA Ops:
  0.0 39.3 %shard_map.100 = bf16[16,1024]{1,0:T(8,128)(2,1)} custom-call(bf16[16,1024]{1,0:T(8,128)(2,1)} %q_hbm.1, bf16[4096,128]{1,0:T(8,128)(2,1)} %ck_hbm.1, bf16[4096,128]{1,0:T(8,128)(2,1)} %cv_hbm.1, bf16[2048,128]{1,0:T(8,128)(2,1)} %tk_hbm.1, bf16[2048,128]{1,0:T(8,128)(2,1)} %tv_hbm.1, bf16[8192,128]{1,0:T(8,128)(2,1)} %hk_hbm.1, bf16[8192,128]{1,0:T(8,128)(2,1)} %hv_hbm.1, ...), custom_call_target="tpu_custom_call" | custom-call | tf_op jit(solution)/shard_map/pallas_call | solution.py:349
  39.3 1.4 %copy.12 = bf16[16,1024]{1,0:T(8,128)(2,1)} copy(bf16[16,1024]{1,0:T(8,128)(2,1)} %shard_map.100) | data formatting | bytes 65536

commit v2 on v1

v2 whole, which is shorter than its diff:
```python
import functools
import math

import jax
import jax.numpy as jnp
from jax import lax
from jax.experimental import pallas as pl
from jax.experimental.pallas import tpu as pltpu
from jax.sharding import PartitionSpec as P

HD = 128
HOLDERS = 2
MESH = pl.DeviceIdType.MESH
F32 = jnp.float32
BF16 = jnp.bfloat16
CS = math.log2(math.e) / math.sqrt(HD)
FAR = 1e30
NT = (((1,), (1,)), ((), ()))
TN = (((0,), (0,)), ((), ()))


def kernel(
    q_hbm,
    ck_hbm,
    cv_hbm,
    tk_hbm,
    tv_hbm,
    hk_hbm,
    hv_hbm,
    len_hbm,
    task_hbm,
    w_hbm,
    out_ref,
    q_all,
    kbuf,
    vbuf,
    vt,
    hkb,
    hvb,
    len_ref,
    task_ref,
    wbuf,
    sa,
    sb,
    pa,
    pb,
    osend,
    orecv,
    xsend,
    xrecv,
    hs,
    hq,
    hot,
    hlse,
    valid,
    psib,
    prib,
    psend,
    precv,
    ld_sem,
    q_send,
    q_recv,
    o_send,
    o_recv,
    x_send,
    x_recv,
    b_send,
    b_recv,
    p_send,
    p_recv,
):
    nreq, rows, width = q_all.shape
    heads = width // HD
    cols = rows * heads
    corpus = ck_hbm.shape[0]
    keys = kbuf.shape[0]
    hist = hkb.shape[0] // rows
    out_w = psend.shape[2]
    chunk, deep = 512, 2048
    nch, ncorp, per = keys // chunk, corpus // chunk, deep // chunk
    me = lax.axis_index("req")
    mj = lax.axis_index("kvh")
    y, x = me // 4, me % 4
    mz, mc = mj // 2, mj % 2

    def off(t):
        dy = 3 - t // 4
        return dy, (t % 4 + 1 + dy) % 4

    def slot(t):
        dy, dx = off(t)
        return dy * 4 + dx

    def peer(t, sign):
        dy, dx = off(t)
        return ((y + 4 + sign * dy) % 4) * 4 + (x + 4 + sign * dx) % 4

    def greet(**device):
        pl.semaphore_signal(
            pltpu.get_barrier_semaphore(), inc=1, device_id=device, device_id_type=MESH
        )

    def greet_req(t, carry):
        greet(req=peer(t, -1))
        return carry

    lax.fori_loop(0, nreq - 1, greet_req, 0)
    greet(kvh=mz * 2 + 1 - mc)
    for dz in range(1, 4):
        greet(kvh=((mz + dz) % 4) * 2 + mc)

    loads = [
        pltpu.make_async_copy(q_hbm, q_all.at[0], ld_sem.at[0]),
        pltpu.make_async_copy(task_hbm, task_ref, ld_sem.at[1]),
        pltpu.make_async_copy(len_hbm, len_ref, ld_sem.at[2]),
        pltpu.make_async_copy(cv_hbm, vbuf.at[pl.ds(0, corpus)], ld_sem.at[3]),
        pltpu.make_async_copy(tv_hbm, vbuf.at[pl.ds(corpus, keys - corpus)], ld_sem.at[4]),
        pltpu.make_async_copy(hk_hbm, hkb, ld_sem.at[5]),
        pltpu.make_async_copy(hv_hbm, hvb, ld_sem.at[6]),
        pltpu.make_async_copy(ck_hbm, kbuf.at[pl.ds(0, corpus)], ld_sem.at[7]),
        pltpu.make_async_copy(tk_hbm, kbuf.at[pl.ds(corpus, keys - corpus)], ld_sem.at[8]),
        pltpu.make_async_copy(w_hbm, wbuf, ld_sem.at[9]),
    ]
    for c in loads:
        c.start()

    loads[1].wait()
    lane = lax.broadcasted_iota(jnp.int32, (nreq, nreq * rows), 1)
    row = lax.broadcasted_iota(jnp.int32, (nreq, nreq * rows), 0)
    mine = jnp.broadcast_to(task_ref[...], lane.shape) == me // HOLDERS
    mine = jnp.where(mine & (lane // rows == row), 1.0, 0.0).astype(BF16)
    er = lax.broadcasted_iota(jnp.int32, (nreq * rows, cols), 0)
    ec = lax.broadcasted_iota(jnp.int32, (nreq * rows, cols), 1)
    spread = jnp.where(er % rows == ec % rows, 1.0, 0.0).astype(BF16)
    valid[...] = jnp.dot(mine, spread, preferred_element_type=F32)

    loads[0].wait()
    pl.semaphore_wait(pltpu.get_barrier_semaphore(), nreq - 1 + 4)

    def q_copy(t):
        return pltpu.make_async_remote_copy(
            src_ref=q_all.at[0],
            dst_ref=q_all.at[slot(t)],
            send_sem=q_send.at[t],
            recv_sem=q_recv.at[t],
            device_id={"req": peer(t, -1)},
            device_id_type=MESH,
        )

    def send_q(t, carry):
        q_copy(t).start()
        return carry

    lax.fori_loop(0, nreq - 1, send_q, 0)

    def head_major(k):
        block = q_all[k]
        return [block[:, h * HD : (h + 1) * HD] for h in range(heads)]

    loads[3].wait()
    loads[4].wait()
    for c in range(nch):
        at = slice(c * chunk, (c + 1) * chunk)
        vt[:HD, at] = vbuf[at, :].T
    vt[HD:, :] = jnp.ones((vt.shape[0] - HD, keys), BF16)

    pr = lax.broadcasted_iota(jnp.int32, (cols, cols), 0)
    pc = lax.broadcasted_iota(jnp.int32, (cols, cols), 1)
    perm = jnp.where((pr % heads == pc // rows) & (pr // heads == pc % rows), 1.0, 0.0)
    perm16 = perm.astype(BF16)
    hq[...] = jnp.dot(perm16, jnp.concatenate(head_major(0), 0), preferred_element_type=F32)
    loads[2].wait()
    loads[5].wait()
    hcol = lax.broadcasted_iota(jnp.int32, (heads, hist), 1)
    for r in range(rows):
        at = slice(r * heads, (r + 1) * heads)
        s = lax.dot_general(
            hq[at, :].astype(BF16),
            hkb[r * hist : (r + 1) * hist, :],
            NT,
            preferred_element_type=F32,
        )
        hs[at, :] = jnp.where(hcol < len_ref[r], s, -FAR)
    s = hs[...]
    hm = jnp.max(s, axis=1, keepdims=True)
    p = jnp.exp2((s - hm) * CS)
    htot = jnp.sum(p, axis=1, keepdims=True)
    hs[...] = p
    loads[6].wait()
    for r in range(rows):
        at = slice(r * heads, (r + 1) * heads)
        hq[at, :] = jnp.dot(
            hs[at, :].astype(BF16), hvb[r * hist : (r + 1) * hist, :], preferred_element_type=F32
        )
    ho = (hq[...] * (1.0 / htot)).astype(BF16)
    hot[...] = lax.dot_general(ho, perm16, TN, preferred_element_type=F32)
    hl = jnp.sum(perm * (hm * CS + jnp.log2(htot)), axis=0, keepdims=True)
    hlse[...] = jnp.broadcast_to(hl, hlse.shape)
    loads[7].wait()
    loads[8].wait()

    def arrive(b):
        for a in range(2):
            t = 2 * b + a
            if isinstance(t, int) and t == nreq - 1:
                continue
            q_copy(t).wait_recv()

    def q_pair(b):
        return jnp.concatenate(head_major(slot(2 * b)) + head_major(slot(2 * b + 1)), 0)

    def score(c, q, sref, peaks):
        at = slice(c * chunk, (c + 1) * chunk)
        s = lax.dot_general(kbuf[at, :], q, NT, preferred_element_type=F32)
        sref[at, :] = s
        part = jnp.max(s.reshape(chunk // 8, 8, 2 * cols), axis=0)
        g = 0 if c < ncorp else 1
        peaks[g] = part if peaks[g] is None else jnp.maximum(peaks[g], part)

    def weigh(c, sref, pref, shifts):
        at = slice(c * chunk, (c + 1) * chunk)
        p = jnp.exp2(sref[at, :] * CS - shifts[0 if c < ncorp else 1])
        pref[at, :] = p.astype(BF16)

    def add_up(g, pref, acc):
        at = slice(g * deep, (g + 1) * deep)
        part = jnp.dot(vt[:, at], pref[at, :], preferred_element_type=F32)
        return part if acc is None else acc + part

    def y_copy(t):
        dy, dx = off(t)
        return pltpu.make_async_remote_copy(
            src_ref=osend.at[slot(t)],
            dst_ref=orecv.at[slot(t)],
            send_sem=o_send.at[t],
            recv_sem=o_recv.at[t],
            device_id={"req": ((y + dy) % 4) * 4 + x},
            device_id_type=MESH,
        )

    def pack(lse):
        hi = lse.astype(BF16).astype(F32)
        mid = (lse - hi).astype(BF16).astype(F32)
        lo = lse - hi - mid
        sub = lax.broadcasted_iota(jnp.int32, (16, lse.shape[1]), 0)
        info = jnp.where(sub == 0, hi, jnp.where(sub == 1, mid, jnp.where(sub == 2, lo, 0.0)))
        return info.astype(BF16)

    def unpack(ref, k):
        lse = jnp.sum(ref[k, HD:, :].astype(F32), axis=0, keepdims=True)
        return ref[k, :HD, :].astype(F32), lse

    def merge(parts):
        top = functools.reduce(jnp.maximum, [v for _, v in parts])
        ws = [jnp.exp2(v - top) for _, v in parts]
        den = functools.reduce(jnp.add, ws)
        inv = 1.0 / den
        o = functools.reduce(jnp.add, [o * (w * inv) for (o, _), w in zip(parts, ws)])
        return o, top + jnp.log2(den)

    def stage(b, s_now, s_next, pref, peaks):
        mask = jnp.concatenate([valid[pl.ds(peer(2 * b + a, 1), 1), :] for a in range(2)], 1) > 0
        pk = [jnp.max(m, axis=0, keepdims=True) for m in peaks]
        top = jnp.maximum(pk[0], jnp.where(mask, pk[1], -FAR)) * CS
        shifts = [top, jnp.where(mask, top, FAR)]
        later = [None, None]
        if s_next is not None:
            arrive(b + 1)
            q = q_pair(b + 1)
        acc, done = None, 0
        for c in range(nch):
            if s_next is not None:
                score(c, q, s_next, later)
            weigh(c, s_now, pref, shifts)
            if (done + 1) * per <= c:
                acc = add_up(done, pref, acc)
                done += 1
        while done * deep < keys:
            acc = add_up(done, pref, acc)
            done += 1
        total = acc[HD : HD + 1, :]
        o = (acc[:HD, :] * (1.0 / total)).astype(BF16)
        info = pack(top + jnp.log2(total))
        for a in range(2):
            t = 2 * b + a
            at = slice(a * cols, (a + 1) * cols)
            osend[slot(t), :HD, :] = o[:, at]
            osend[slot(t), HD:, :] = info[:, at]
            if not isinstance(t, int) or t < nreq - 4:
                y_copy(t).start()
        return later

    arrive(0)
    peaks = [None, None]
    q0 = q_pair(0)
    for c in range(nch):
        score(c, q0, sa, peaks)

    def twice(i, peaks):
        peaks = stage(2 * i, sa, sb, pa, list(peaks))
        peaks = stage(2 * i + 1, sb, sa, pb, peaks)
        return tuple(peaks)

    nb = nreq // 2
    peaks = list(lax.fori_loop(0, nb // 2 - 1, twice, tuple(peaks)))
    peaks = stage(nb - 2, sa, sb, pa, peaks)
    stage(nb - 1, sb, None, pb, peaks)

    def y_arrived(t, carry):
        y_copy(t).wait_recv()
        return carry

    lax.fori_loop(0, nreq - 4, y_arrived, 0)

    def x_copy(dx):
        return pltpu.make_async_remote_copy(
            src_ref=xsend.at[dx],
            dst_ref=xrecv.at[dx],
            send_sem=x_send.at[dx],
            recv_sem=x_recv.at[dx],
            device_id={"req": y * 4 + (x + dx) % 4},
            device_id_type=MESH,
        )

    def along_y(dx):
        return merge([unpack(osend, dx)] + [unpack(orecv, dy * 4 + dx) for dy in range(1, 4)])

    for dx in (2, 1, 3):
        o, lse = along_y(dx)
        xsend[dx, :HD, :] = o.astype(BF16)
        xsend[dx, HD:, :] = pack(lse)
        x_copy(dx).start()
    home = merge([along_y(0), (hot[...], hlse[0:1, :])])
    for dx in (1, 3, 2):
        x_copy(dx).wait_recv()
    att, _ = merge([home] + [unpack(xrecv, dx) for dx in range(1, 4)])
    att = att.T.astype(BF16)
    att = jnp.concatenate([att[h * rows : (h + 1) * rows, :] for h in range(heads)], 1)

    loads[9].wait()

    def project(z, c):
        at = pl.ds(pl.multiple_of((z * 2 + c) * out_w, out_w), out_w)
        return jnp.dot(att, wbuf[:, at], preferred_element_type=F32)

    def b_copy(dz):
        return pltpu.make_async_remote_copy(
            src_ref=psib.at[dz],
            dst_ref=prib.at[dz],
            send_sem=b_send.at[dz],
            recv_sem=b_recv.at[dz],
            device_id={"kvh": mz * 2 + 1 - mc},
            device_id_type=MESH,
        )

    def p_copy(dz):
        return pltpu.make_async_remote_copy(
            src_ref=psend.at[dz],
            dst_ref=precv.at[dz],
            send_sem=p_send.at[dz],
            recv_sem=p_recv.at[dz],
            device_id={"kvh": ((mz + dz) % 4) * 2 + mc},
            device_id_type=MESH,
        )

    def give(i, carry):
        dz = (2 + i) % 4
        psib[dz] = project((mz + dz) % 4, 1 - mc).astype(BF16)
        b_copy(dz).start()
        return carry

    lax.fori_loop(0, 4, give, 0)

    def both(dz):
        own = project((mz + dz) % 4, mc)
        b_copy(dz).wait_recv()
        return own + prib[dz].astype(F32)

    def forward(i, carry):
        dz = 2 + i - 3 * (i // 2)
        psend[dz] = both(dz).astype(BF16)
        p_copy(dz).start()
        return carry

    lax.fori_loop(0, 3, forward, 0)
    mixed = both(0)
    for dz in (3, 1, 2):
        p_copy(dz).wait_recv()
        mixed = mixed + precv[dz].astype(F32)
    out_ref[...] = mixed.astype(BF16)

    def q_sent(t, carry):
        q_copy(t).wait_send()
        return carry

    lax.fori_loop(0, nreq - 1, q_sent, 0)

    def y_sent(t, carry):
        y_copy(t).wait_send()
        return carry

    lax.fori_loop(0, nreq - 4, y_sent, 0)
    for d in range(1, 4):
        x_copy(d).wait_send()
        p_copy(d).wait_send()
    for d in range(4):
        b_copy(d).wait_send()


def solution(mesh):
    nreq, nkv = mesh.shape["req"], mesh.shape["kvh"]

    def shards(q, ck, cv, tk, tv, hk, hv, lengths, task_of, w):
        rows, width = q.shape
        cols = rows * (width // HD)
        keys = ck.shape[0] + tk.shape[0]
        hist = hk.shape[0] // rows
        out_w = w.shape[1] // nkv
        hbm = pl.BlockSpec(memory_space=pl.ANY)
        vmem = pl.BlockSpec(memory_space=pltpu.VMEM)
        dma = pltpu.SemaphoreType.DMA
        return pl.pallas_call(
            kernel,
            out_shape=jax.ShapeDtypeStruct((rows, out_w), BF16),
            in_specs=[hbm] * 10,
            out_specs=vmem,
            scratch_shapes=[
                pltpu.VMEM((nreq, rows, width), BF16),
                pltpu.VMEM((keys, HD), BF16),
                pltpu.VMEM((keys, HD), BF16),
                pltpu.VMEM((HD + 16, keys), BF16),
                pltpu.VMEM(hk.shape, BF16),
                pltpu.VMEM(hv.shape, BF16),
                pltpu.SMEM(lengths.shape, jnp.int32),
                pltpu.VMEM((1, nreq * rows), jnp.int32),
                pltpu.VMEM(w.shape, BF16),
                pltpu.VMEM((keys, 2 * cols), F32),
                pltpu.VMEM((keys, 2 * cols), F32),
                pltpu.VMEM((keys, 2 * cols), BF16),
                pltpu.VMEM((keys, 2 * cols), BF16),
                pltpu.VMEM((nreq, HD + 16, cols), BF16),
                pltpu.VMEM((nreq, HD + 16, cols), BF16),
                pltpu.VMEM((4, HD + 16, cols), BF16),
                pltpu.VMEM((4, HD + 16, cols), BF16),
                pltpu.VMEM((cols, hist), F32),
                pltpu.VMEM((cols, HD), F32),
                pltpu.VMEM((HD, cols), F32),
                pltpu.VMEM((8, cols), F32),
                pltpu.VMEM((nreq, cols), F32),
                pltpu.VMEM((4, rows, out_w), BF16),
                pltpu.VMEM((4, rows, out_w), BF16),
                pltpu.VMEM((4, rows, out_w), BF16),
                pltpu.VMEM((4, rows, out_w), BF16),
                dma((10,)),
                dma((nreq,)),
                dma((nreq,)),
                dma((nreq,)),
                dma((nreq,)),
                dma((4,)),
                dma((4,)),
                dma((4,)),
                dma((4,)),
                dma((4,)),
                dma((4,)),
            ],
            compiler_params=pltpu.CompilerParams(
                collective_id=0, has_side_effects=True, vmem_limit_bytes=60 * 2**20
            ),
        )(q, ck, cv, tk, tv, hk, hv, lengths, task_of.reshape(1, -1), w)

    return jax.shard_map(
        shards,
        mesh=mesh,
        in_specs=(P("req", "kvh"),) * 7 + (P("req"), P(), P("kvh", None)),
        out_specs=P("req", "kvh"),
        check_vma=False,
    )
```

time: 40.9 us -> 41.8 us (1.022)
  Pallas kernels: 39.3 us -> 40.3 us
    pallas_call x1, Pallas kernels: 39.3 us -> 40.3 us  [shards(): pl.pallas_call(kernel, out_shape=jax.ShapeDtypeStruct((rows, out_w), BF16...]
where the time goes in v2:
time: 41.8 us; the launch traced here: 41.6 us
  Pallas kernels  40.3 us (96%)
  local copies, waits for them, and re-layouts  1.38 us (3%)
    pallas_call x1, Pallas kernels, shards(): pl.pallas_call(kernel, out_shape=jax.ShapeDtypeStruct((rows, out_w), BF16...  40.3 us
    unnamed x1, local copies, waits for them, and re-layouts  1.38 us

profile of v2, /device:TPU:1, one launch (start us, length us, event | category | flops | bytes accessed | tf_op | source)
XLA Modules:
  0.0 41.6 jit_solution(11595590795307604623)
XLA Ops:
  0.0 40.3 %shard_map.100 = bf16[16,1024]{1,0:T(8,128)(2,1)} custom-call(bf16[16,1024]{1,0:T(8,128)(2,1)} %q_hbm.1, bf16[4096,128]{1,0:T(8,128)(2,1)} %ck_hbm.1, bf16[4096,128]{1,0:T(8,128)(2,1)} %cv_hbm.1, bf16[2048,128]{1,0:T(8,128)(2,1)} %tk_hbm.1, bf16[2048,128]{1,0:T(8,128)(2,1)} %tv_hbm.1, bf16[8192,128]{1,0:T(8,128)(2,1)} %hk_hbm.1, bf16[8192,128]{1,0:T(8,128)(2,1)} %hv_hbm.1, ...), custom_call_target="tpu_custom_call" | custom-call | tf_op jit(solution)/shard_map/pallas_call | solution.py:422
  40.3 1.4 %copy.12 = bf16[16,1024]{1,0:T(8,128)(2,1)} copy(bf16[16,1024]{1,0:T(8,128)(2,1)} %shard_map.100) | data formatting | bytes 65536

commit v3 on v2

v3 whole, which is shorter than its diff:
```python
import functools
import math

import jax
import jax.numpy as jnp
from jax import lax
from jax.experimental import pallas as pl
from jax.experimental.pallas import tpu as pltpu
from jax.sharding import PartitionSpec as P

HD = 128
HOLDERS = 2
MESH = pl.DeviceIdType.MESH
F32 = jnp.float32
BF16 = jnp.bfloat16
CS = math.log2(math.e) / math.sqrt(HD)
FAR = 1e30
NT = (((1,), (1,)), ((), ()))
TN = (((0,), (0,)), ((), ()))


def kernel(
    q_hbm,
    ck_hbm,
    cv_hbm,
    tk_hbm,
    tv_hbm,
    hk_hbm,
    hv_hbm,
    len_hbm,
    task_hbm,
    w_hbm,
    out_ref,
    q_all,
    kbuf,
    vbuf,
    vt,
    hkb,
    hvb,
    len_ref,
    task_ref,
    wbuf,
    sa,
    sb,
    pa,
    pb,
    osend,
    orecv,
    hs,
    hq,
    valid,
    psend,
    precv,
    ld_sem,
    q_send,
    q_recv,
    o_send,
    o_recv,
    p_send,
    p_recv,
):
    nreq, rows, width = q_all.shape
    nkv = psend.shape[0]
    heads = width // HD
    cols = rows * heads
    corpus = ck_hbm.shape[0]
    keys = kbuf.shape[0]
    hist = hkb.shape[0] // rows
    out_w = psend.shape[2]
    chunk, deep = 512, 2048
    nch, ncorp, per = keys // chunk, corpus // chunk, deep // chunk
    me = lax.axis_index("req")
    mj = lax.axis_index("kvh")
    y, x = me // 4, me % 4
    mz, mc = mj // 2, mj % 2

    def off(t):
        dy = 3 - t // 4
        return dy, (t % 4 + 1 + dy) % 4

    def slot(t):
        dy, dx = off(t)
        return dy * 4 + dx

    def peer(t, sign):
        dy, dx = off(t)
        return ((y + 4 + sign * dy) % 4) * 4 + (x + 4 + sign * dx) % 4

    def greet(**device):
        pl.semaphore_signal(
            pltpu.get_barrier_semaphore(), inc=1, device_id=device, device_id_type=MESH
        )

    def greet_req(t, carry):
        greet(req=peer(t, -1))
        return carry

    lax.fori_loop(0, nreq - 1, greet_req, 0)

    def greet_kv(e, carry):
        greet(kvh=(mj + e) % nkv)
        return carry

    lax.fori_loop(1, nkv, greet_kv, 0)

    loads = [
        pltpu.make_async_copy(q_hbm, q_all.at[0], ld_sem.at[0]),
        pltpu.make_async_copy(task_hbm, task_ref, ld_sem.at[1]),
        pltpu.make_async_copy(len_hbm, len_ref, ld_sem.at[2]),
        pltpu.make_async_copy(cv_hbm, vbuf.at[pl.ds(0, corpus)], ld_sem.at[3]),
        pltpu.make_async_copy(tv_hbm, vbuf.at[pl.ds(corpus, keys - corpus)], ld_sem.at[4]),
        pltpu.make_async_copy(ck_hbm, kbuf.at[pl.ds(0, corpus)], ld_sem.at[5]),
        pltpu.make_async_copy(tk_hbm, kbuf.at[pl.ds(corpus, keys - corpus)], ld_sem.at[6]),
        pltpu.make_async_copy(hk_hbm, hkb, ld_sem.at[7]),
        pltpu.make_async_copy(hv_hbm, hvb, ld_sem.at[8]),
        pltpu.make_async_copy(w_hbm, wbuf, ld_sem.at[9]),
    ]
    for c in loads:
        c.start()

    loads[0].wait()
    pl.semaphore_wait(pltpu.get_barrier_semaphore(), nreq + nkv - 2)

    def q_copy(t):
        return pltpu.make_async_remote_copy(
            src_ref=q_all.at[0],
            dst_ref=q_all.at[slot(t)],
            send_sem=q_send.at[t],
            recv_sem=q_recv.at[t],
            device_id={"req": peer(t, -1)},
            device_id_type=MESH,
        )

    def send_q(t, carry):
        q_copy(t).start()
        return carry

    lax.fori_loop(0, nreq - 1, send_q, 0)

    def head_major(k):
        block = q_all[k]
        return [block[:, h * HD : (h + 1) * HD] for h in range(heads)]

    loads[1].wait()
    lane = lax.broadcasted_iota(jnp.int32, (nreq, nreq * rows), 1)
    row = lax.broadcasted_iota(jnp.int32, (nreq, nreq * rows), 0)
    mine = jnp.broadcast_to(task_ref[...], lane.shape) == me // HOLDERS
    mine = jnp.where(mine & (lane // rows == row), 1.0, 0.0).astype(BF16)
    er = lax.broadcasted_iota(jnp.int32, (nreq * rows, cols), 0)
    ec = lax.broadcasted_iota(jnp.int32, (nreq * rows, cols), 1)
    spread = jnp.where(er % rows == ec % rows, 1.0, 0.0).astype(BF16)
    valid[...] = jnp.dot(mine, spread, preferred_element_type=F32)

    loads[3].wait()
    loads[4].wait()
    for c in range(nch):
        at = slice(c * chunk, (c + 1) * chunk)
        vt[:HD, at] = vbuf[at, :].T
    vt[HD:, :] = jnp.ones((vt.shape[0] - HD, keys), BF16)
    loads[5].wait()
    loads[6].wait()

    def arrive(b):
        for a in range(2):
            t = 2 * b + a
            if isinstance(t, int) and t == nreq - 1:
                continue
            q_copy(t).wait_recv()

    def q_pair(b):
        return jnp.concatenate(head_major(slot(2 * b)) + head_major(slot(2 * b + 1)), 0)

    def score(c, q, sref, peaks):
        at = slice(c * chunk, (c + 1) * chunk)
        s = lax.dot_general(kbuf[at, :], q, NT, preferred_element_type=F32)
        sref[at, :] = s
        part = jnp.max(s.reshape(chunk // 8, 8, 2 * cols), axis=0)
        g = 0 if c < ncorp else 1
        peaks[g] = part if peaks[g] is None else jnp.maximum(peaks[g], part)

    def weigh(c, sref, pref, shifts):
        at = slice(c * chunk, (c + 1) * chunk)
        p = jnp.exp2(sref[at, :] * CS - shifts[0 if c < ncorp else 1])
        pref[at, :] = p.astype(BF16)

    def add_up(g, pref, acc):
        at = slice(g * deep, (g + 1) * deep)
        part = jnp.dot(vt[:, at], pref[at, :], preferred_element_type=F32)
        return part if acc is None else acc + part

    def o_copy(t):
        return pltpu.make_async_remote_copy(
            src_ref=osend.at[t],
            dst_ref=orecv.at[t],
            send_sem=o_send.at[t],
            recv_sem=o_recv.at[t],
            device_id={"req": peer(t, 1)},
            device_id_type=MESH,
        )

    def pack(lse):
        hi = lse.astype(BF16).astype(F32)
        mid = (lse - hi).astype(BF16).astype(F32)
        lo = lse - hi - mid
        sub = lax.broadcasted_iota(jnp.int32, (16, lse.shape[1]), 0)
        info = jnp.where(sub == 0, hi, jnp.where(sub == 1, mid, jnp.where(sub == 2, lo, 0.0)))
        return info.astype(BF16)

    def unpack(ref, k):
        lse = jnp.sum(ref[k, HD:, :].astype(F32), axis=0, keepdims=True)
        return ref[k, :HD, :].astype(F32), lse

    def merge(parts):
        top = functools.reduce(jnp.maximum, [v for _, v in parts])
        ws = [jnp.exp2(v - top) for _, v in parts]
        den = functools.reduce(jnp.add, ws)
        inv = 1.0 / den
        o = functools.reduce(jnp.add, [o * (w * inv) for (o, _), w in zip(parts, ws)])
        return o, top + jnp.log2(den)

    def stage(b, s_now, s_next, pref, peaks):
        mask = jnp.concatenate([valid[pl.ds(peer(2 * b + a, 1), 1), :] for a in range(2)], 1) > 0
        pk = [jnp.max(m, axis=0, keepdims=True) for m in peaks]
        top = jnp.maximum(pk[0], jnp.where(mask, pk[1], -FAR)) * CS
        shifts = [top, jnp.where(mask, top, FAR)]
        later = [None, None]
        if s_next is not None:
            arrive(b + 1)
            q = q_pair(b + 1)
        acc, done = None, 0
        for c in range(nch):
            if s_next is not None:
                score(c, q, s_next, later)
            weigh(c, s_now, pref, shifts)
            if (done + 1) * per <= c:
                acc = add_up(done, pref, acc)
                done += 1
        while done * deep < keys:
            acc = add_up(done, pref, acc)
            done += 1
        total = acc[HD : HD + 1, :]
        o = (acc[:HD, :] * (1.0 / total)).astype(BF16)
        info = pack(top + jnp.log2(total))
        for a in range(2):
            t = 2 * b + a
            at = slice(a * cols, (a + 1) * cols)
            osend[t, :HD, :] = o[:, at]
            osend[t, HD:, :] = info[:, at]
            if not isinstance(t, int) or t < nreq - 1:
                o_copy(t).start()
        return later

    arrive(0)
    peaks = [None, None]
    q0 = q_pair(0)
    for c in range(nch):
        score(c, q0, sa, peaks)

    def twice(i, peaks):
        peaks = stage(2 * i, sa, sb, pa, list(peaks))
        peaks = stage(2 * i + 1, sb, sa, pb, peaks)
        return tuple(peaks)

    nb = nreq // 2
    peaks = list(lax.fori_loop(0, nb // 2 - 1, twice, tuple(peaks)))
    peaks = stage(nb - 2, sa, sb, pa, peaks)
    stage(nb - 1, sb, None, pb, peaks)

    pr = lax.broadcasted_iota(jnp.int32, (cols, cols), 0)
    pc = lax.broadcasted_iota(jnp.int32, (cols, cols), 1)
    perm = jnp.where((pr % heads == pc // rows) & (pr // heads == pc % rows), 1.0, 0.0)
    perm16 = perm.astype(BF16)
    hq[...] = jnp.dot(perm16, jnp.concatenate(head_major(0), 0), preferred_element_type=F32)
    loads[2].wait()
    loads[7].wait()
    hcol = lax.broadcasted_iota(jnp.int32, (heads, hist), 1)
    for r in range(rows):
        at = slice(r * heads, (r + 1) * heads)
        s = lax.dot_general(
            hq[at, :].astype(BF16),
            hkb[r * hist : (r + 1) * hist, :],
            NT,
            preferred_element_type=F32,
        )
        hs[at, :] = jnp.where(hcol < len_ref[r], s, -FAR)
    s = hs[...]
    hm = jnp.max(s, axis=1, keepdims=True)
    p = jnp.exp2((s - hm) * CS)
    htot = jnp.sum(p, axis=1, keepdims=True)
    hs[...] = p
    loads[8].wait()
    for r in range(rows):
        at = slice(r * heads, (r + 1) * heads)
        hq[at, :] = jnp.dot(
            hs[at, :].astype(BF16), hvb[r * hist : (r + 1) * hist, :], preferred_element_type=F32
        )
    ho = (hq[...] * (1.0 / htot)).astype(BF16)
    hot = lax.dot_general(ho, perm16, TN, preferred_element_type=F32)
    hl = jnp.sum(perm * (hm * CS + jnp.log2(htot)), axis=0, keepdims=True)

    early = nreq - 4

    def arrived(t, carry):
        o_copy(t).wait_recv()
        return carry

    lax.fori_loop(0, early, arrived, 0)
    home = merge(
        [unpack(osend, nreq - 1), (hot, hl)] + [unpack(orecv, t) for t in range(early)]
    )
    lax.fori_loop(early, nreq - 1, arrived, 0)
    att, _ = merge([home] + [unpack(orecv, t) for t in range(early, nreq - 1)])
    att = att.T.astype(BF16)
    att = jnp.concatenate([att[h * rows : (h + 1) * rows, :] for h in range(heads)], 1)

    loads[9].wait()

    def kv_peer(e):
        dz, dc = e // 2, e % 2
        dz = dz + dz // 2 - 2 * (dz // 3)
        return ((mz + dz) % 4) * 2 + (mc + dc) % 2

    def p_copy(e):
        return pltpu.make_async_remote_copy(
            src_ref=psend.at[e],
            dst_ref=precv.at[e],
            send_sem=p_send.at[e],
            recv_sem=p_recv.at[e],
            device_id={"kvh": kv_peer(e)},
            device_id_type=MESH,
        )

    def project(e):
        at = pl.ds(pl.multiple_of(kv_peer(e) * out_w, out_w), out_w)
        return jnp.dot(att, wbuf[:, at], preferred_element_type=F32)

    def send_p(i, carry):
        e = nkv - 1 - i
        psend[e] = project(e).astype(BF16)
        p_copy(e).start()
        return carry

    lax.fori_loop(0, nkv - 1, send_p, 0)
    mixed = project(0)
    for e in (7, 6, 1, 5, 4, 3, 2):
        p_copy(e).wait_recv()
        mixed = mixed + precv[e].astype(F32)
    out_ref[...] = mixed.astype(BF16)

    def sent(t, carry):
        q_copy(t).wait_send()
        o_copy(t).wait_send()
        return carry

    lax.fori_loop(0, nreq - 1, sent, 0)

    def p_sent(e, carry):
        p_copy(e).wait_send()
        return carry

    lax.fori_loop(1, nkv, p_sent, 0)


def solution(mesh):
    nreq, nkv = mesh.shape["req"], mesh.shape["kvh"]

    def shards(q, ck, cv, tk, tv, hk, hv, lengths, task_of, w):
        rows, width = q.shape
        cols = rows * (width // HD)
        keys = ck.shape[0] + tk.shape[0]
        hist = hk.shape[0] // rows
        out_w = w.shape[1] // nkv
        hbm = pl.BlockSpec(memory_space=pl.ANY)
        vmem = pl.BlockSpec(memory_space=pltpu.VMEM)
        dma = pltpu.SemaphoreType.DMA
        return pl.pallas_call(
            kernel,
            out_shape=jax.ShapeDtypeStruct((rows, out_w), BF16),
            in_specs=[hbm] * 10,
            out_specs=vmem,
            scratch_shapes=[
                pltpu.VMEM((nreq, rows, width), BF16),
                pltpu.VMEM((keys, HD), BF16),
                pltpu.VMEM((keys, HD), BF16),
                pltpu.VMEM((HD + 16, keys), BF16),
                pltpu.VMEM(hk.shape, BF16),
                pltpu.VMEM(hv.shape, BF16),
                pltpu.SMEM(lengths.shape, jnp.int32),
                pltpu.VMEM((1, nreq * rows), jnp.int32),
                pltpu.VMEM(w.shape, BF16),
                pltpu.VMEM((keys, 2 * cols), F32),
                pltpu.VMEM((keys, 2 * cols), F32),
                pltpu.VMEM((keys, 2 * cols), BF16),
                pltpu.VMEM((keys, 2 * cols), BF16),
                pltpu.VMEM((nreq, HD + 16, cols), BF16),
                pltpu.VMEM((nreq, HD + 16, cols), BF16),
                pltpu.VMEM((cols, hist), F32),
                pltpu.VMEM((cols, HD), F32),
                pltpu.VMEM((nreq, cols), F32),
                pltpu.VMEM((nkv, rows, out_w), BF16),
                pltpu.VMEM((nkv, rows, out_w), BF16),
                dma((10,)),
                dma((nreq,)),
                dma((nreq,)),
                dma((nreq,)),
                dma((nreq,)),
                dma((nkv,)),
                dma((nkv,)),
            ],
            compiler_params=pltpu.CompilerParams(
                collective_id=0, has_side_effects=True, vmem_limit_bytes=60 * 2**20
            ),
        )(q, ck, cv, tk, tv, hk, hv, lengths, task_of.reshape(1, -1), w)

    return jax.shard_map(
        shards,
        mesh=mesh,
        in_specs=(P("req", "kvh"),) * 7 + (P("req"), P(), P("kvh", None)),
        out_specs=P("req", "kvh"),
        check_vma=False,
    )
```

time: 41.8 us -> 40.3 us (0.964)
  Pallas kernels: 40.3 us -> 38.7 us
    pallas_call x1, Pallas kernels: 40.3 us -> 38.7 us  [shards(): pl.pallas_call(kernel, out_shape=jax.ShapeDtypeStruct((rows, out_w), BF16...]
where the time goes in v3:
time: 40.3 us; the launch traced here: 40.1 us
  Pallas kernels  38.7 us (96%)
  local copies, waits for them, and re-layouts  1.38 us (3%)
    pallas_call x1, Pallas kernels, shards(): pl.pallas_call(kernel, out_shape=jax.ShapeDtypeStruct((rows, out_w), BF16...  38.7 us
    unnamed x1, local copies, waits for them, and re-layouts  1.38 us

profile of v3, /device:TPU:1, one launch (start us, length us, event | category | flops | bytes accessed | tf_op | source)
XLA Modules:
  0.0 40.1 jit_solution(6760230707962907330)
XLA Ops:
  0.0 38.7 %shard_map.100 = bf16[16,1024]{1,0:T(8,128)(2,1)} custom-call(bf16[16,1024]{1,0:T(8,128)(2,1)} %q_hbm.1, bf16[4096,128]{1,0:T(8,128)(2,1)} %ck_hbm.1, bf16[4096,128]{1,0:T(8,128)(2,1)} %cv_hbm.1, bf16[2048,128]{1,0:T(8,128)(2,1)} %tk_hbm.1, bf16[2048,128]{1,0:T(8,128)(2,1)} %tv_hbm.1, bf16[8192,128]{1,0:T(8,128)(2,1)} %hk_hbm.1, bf16[8192,128]{1,0:T(8,128)(2,1)} %hv_hbm.1, ...), custom_call_target="tpu_custom_call" | custom-call | tf_op jit(solution)/shard_map/pallas_call | solution.py:376
  38.7 1.4 %copy.12 = bf16[16,1024]{1,0:T(8,128)(2,1)} copy(bf16[16,1024]{1,0:T(8,128)(2,1)} %shard_map.100) | data formatting | bytes 65536

commit v4 on v3

--- a/solution.py
+++ b/solution.py
@@ -50,7 +50,6 @@
     hq,
     valid,
     psend,
-    precv,
     ld_sem,
     q_send,
     q_recv,
@@ -125,7 +124,7 @@
         return pltpu.make_async_remote_copy(
             src_ref=q_all.at[0],
             dst_ref=q_all.at[slot(t)],
-            send_sem=q_send.at[t],
+            send_sem=q_send,
             recv_sem=q_recv.at[t],
             device_id={"req": peer(t, -1)},
             device_id_type=MESH,
@@ -160,40 +159,40 @@
     loads[5].wait()
     loads[6].wait()
 
-    def arrive(b):
-        for a in range(2):
-            t = 2 * b + a
-            if isinstance(t, int) and t == nreq - 1:
-                continue
+    early = nreq - 4
+
+    def arrive(block):
+        for t in block:
             q_copy(t).wait_recv()
 
-    def q_pair(b):
-        return jnp.concatenate(head_major(slot(2 * b)) + head_major(slot(2 * b + 1)), 0)
+    def q_of(block):
+        return jnp.concatenate([tile for t in block for tile in head_major(slot(t))], 0)
 
     def score(c, q, sref, peaks):
         at = slice(c * chunk, (c + 1) * chunk)
         s = lax.dot_general(kbuf[at, :], q, NT, preferred_element_type=F32)
-        sref[at, :] = s
-        part = jnp.max(s.reshape(chunk // 8, 8, 2 * cols), axis=0)
+        sref[at, : s.shape[1]] = s
+        part = jnp.max(s.reshape(chunk // 8, 8, s.shape[1]), axis=0)
         g = 0 if c < ncorp else 1
         peaks[g] = part if peaks[g] is None else jnp.maximum(peaks[g], part)
 
     def weigh(c, sref, pref, shifts):
         at = slice(c * chunk, (c + 1) * chunk)
-        p = jnp.exp2(sref[at, :] * CS - shifts[0 if c < ncorp else 1])
-        pref[at, :] = p.astype(BF16)
-
-    def add_up(g, pref, acc):
+        n = shifts[0].shape[1]
+        p = jnp.exp2(sref[at, :n] * CS - shifts[0 if c < ncorp else 1])
+        pref[at, :n] = p.astype(BF16)
+
+    def add_up(g, pref, n, acc):
         at = slice(g * deep, (g + 1) * deep)
-        part = jnp.dot(vt[:, at], pref[at, :], preferred_element_type=F32)
+        part = jnp.dot(vt[:, at], pref[at, :n], preferred_element_type=F32)
         return part if acc is None else acc + part
 
     def o_copy(t):
         return pltpu.make_async_remote_copy(
             src_ref=osend.at[t],
             dst_ref=orecv.at[t],
-            send_sem=o_send.at[t],
-            recv_sem=o_recv.at[t],
+            send_sem=o_send,
+            recv_sem=o_recv.at[t // early],
             device_id={"req": peer(t, 1)},
             device_id_type=MESH,
         )
@@ -218,31 +217,31 @@
         o = functools.reduce(jnp.add, [o * (w * inv) for (o, _), w in zip(parts, ws)])
         return o, top + jnp.log2(den)
 
-    def stage(b, s_now, s_next, pref, peaks):
-        mask = jnp.concatenate([valid[pl.ds(peer(2 * b + a, 1), 1), :] for a in range(2)], 1) > 0
+    def stage(now, then, s_now, s_then, pref, peaks):
+        n = len(now) * cols
+        mask = jnp.concatenate([valid[pl.ds(peer(t, 1), 1), :] for t in now], 1) > 0
         pk = [jnp.max(m, axis=0, keepdims=True) for m in peaks]
         top = jnp.maximum(pk[0], jnp.where(mask, pk[1], -FAR)) * CS
         shifts = [top, jnp.where(mask, top, FAR)]
         later = [None, None]
-        if s_next is not None:
-            arrive(b + 1)
-            q = q_pair(b + 1)
+        if then:
+            arrive(then)
+            q = q_of(then)
         acc, done = None, 0
         for c in range(nch):
-            if s_next is not None:
-                score(c, q, s_next, later)
+            if then:
+                score(c, q, s_then, later)
             weigh(c, s_now, pref, shifts)
             if (done + 1) * per <= c:
-                acc = add_up(done, pref, acc)
+                acc = add_up(done, pref, n, acc)
                 done += 1
         while done * deep < keys:
-            acc = add_up(done, pref, acc)
+            acc = add_up(done, pref, n, acc)
             done += 1
         total = acc[HD : HD + 1, :]
         o = (acc[:HD, :] * (1.0 / total)).astype(BF16)
         info = pack(top + jnp.log2(total))
-        for a in range(2):
-            t = 2 * b + a
+        for a, t in enumerate(now):
             at = slice(a * cols, (a + 1) * cols)
             osend[t, :HD, :] = o[:, at]
             osend[t, HD:, :] = info[:, at]
@@ -250,21 +249,14 @@
                 o_copy(t).start()
         return later
 
-    arrive(0)
-    peaks = [None, None]
-    q0 = q_pair(0)
-    for c in range(nch):
-        score(c, q0, sa, peaks)
-
-    def twice(i, peaks):
-        peaks = stage(2 * i, sa, sb, pa, list(peaks))
-        peaks = stage(2 * i + 1, sb, sa, pb, peaks)
-        return tuple(peaks)
-
-    nb = nreq // 2
-    peaks = list(lax.fori_loop(0, nb // 2 - 1, twice, tuple(peaks)))
-    peaks = stage(nb - 2, sa, sb, pa, peaks)
-    stage(nb - 1, sb, None, pb, peaks)
+    def first_scores(block, sref):
+        peaks = [None, None]
+        q = q_of(block)
+        for c in range(nch):
+            score(c, q, sref, peaks)
+        return peaks
+
+    stage([nreq - 1], None, sb, None, pb, first_scores([nreq - 1], sb))
 
     pr = lax.broadcasted_iota(jnp.int32, (cols, cols), 0)
     pc = lax.broadcasted_iota(jnp.int32, (cols, cols), 1)
@@ -298,17 +290,34 @@
     hot = lax.dot_general(ho, perm16, TN, preferred_element_type=F32)
     hl = jnp.sum(perm * (hm * CS + jnp.log2(htot)), axis=0, keepdims=True)
 
-    early = nreq - 4
-
-    def arrived(t, carry):
-        o_copy(t).wait_recv()
-        return carry
-
-    lax.fori_loop(0, early, arrived, 0)
+    arrive([0, 1])
+    peaks = first_scores([0, 1], sa)
+
+    def twice(i, peaks):
+        t = 4 * i
+        peaks = stage([t, t + 1], [t + 2, t + 3], sa, sb, pa, list(peaks))
+        peaks = stage([t + 2, t + 3], [t + 4, t + 5], sb, sa, pb, peaks)
+        return tuple(peaks)
+
+    peaks = list(lax.fori_loop(0, nreq // 4 - 1, twice, tuple(peaks)))
+    peaks = stage([nreq - 4, nreq - 3], [nreq - 2], sa, sb, pa, peaks)
+    stage([nreq - 2], None, sb, None, pb, peaks)
+
+    def arrived(t, n):
+        pltpu.make_async_remote_copy(
+            src_ref=osend.at[pl.ds(t, n)],
+            dst_ref=orecv.at[pl.ds(t, n)],
+            send_sem=o_send,
+            recv_sem=o_recv.at[t // early],
+            device_id={"req": peer(0, 1)},
+            device_id_type=MESH,
+        ).wait_recv()
+
+    arrived(0, early)
     home = merge(
         [unpack(osend, nreq - 1), (hot, hl)] + [unpack(orecv, t) for t in range(early)]
     )
-    lax.fori_loop(early, nreq - 1, arrived, 0)
+    arrived(early, 3)
     att, _ = merge([home] + [unpack(orecv, t) for t in range(early, nreq - 1)])
     att = att.T.astype(BF16)
     att = jnp.concatenate([att[h * rows : (h + 1) * rows, :] for h in range(heads)], 1)
@@ -323,9 +332,9 @@
     def p_copy(e):
         return pltpu.make_async_remote_copy(
             src_ref=psend.at[e],
-            dst_ref=precv.at[e],
-            send_sem=p_send.at[e],
-            recv_sem=p_recv.at[e],
+            dst_ref=out_ref.at[e],
+            send_sem=p_send,
+            recv_sem=p_recv,
             device_id={"kvh": kv_peer(e)},
             device_id_type=MESH,
         )
@@ -341,24 +350,27 @@
         return carry
 
     lax.fori_loop(0, nkv - 1, send_p, 0)
-    mixed = project(0)
-    for e in (7, 6, 1, 5, 4, 3, 2):
-        p_copy(e).wait_recv()
-        mixed = mixed + precv[e].astype(F32)
-    out_ref[...] = mixed.astype(BF16)
-
-    def sent(t, carry):
-        q_copy(t).wait_send()
-        o_copy(t).wait_send()
-        return carry
-
-    lax.fori_loop(0, nreq - 1, sent, 0)
-
-    def p_sent(e, carry):
-        p_copy(e).wait_send()
-        return carry
-
-    lax.fori_loop(1, nkv, p_sent, 0)
+    psend[0] = project(0).astype(BF16)
+    keep = pltpu.make_async_copy(psend.at[0], out_ref.at[0], ld_sem.at[1])
+    keep.start()
+
+    def whole(src, dst, send_sem, recv_sem):
+        return pltpu.make_async_remote_copy(
+            src_ref=src,
+            dst_ref=dst,
+            send_sem=send_sem,
+            recv_sem=recv_sem,
+            device_id={"kvh": kv_peer(1)},
+            device_id_type=MESH,
+        )
+
+    others = pl.ds(1, nreq - 1)
+    whole(q_all.at[others], q_all.at[others], q_send, q_recv.at[0]).wait_send()
+    whole(osend.at[others], orecv.at[others], o_send, o_recv.at[0]).wait_send()
+    parts = whole(psend.at[pl.ds(1, nkv - 1)], out_ref.at[pl.ds(1, nkv - 1)], p_send, p_recv)
+    parts.wait_send()
+    parts.wait_recv()
+    keep.wait()
 
 
 def solution(mesh):
@@ -371,13 +383,12 @@
         hist = hk.shape[0] // rows
         out_w = w.shape[1] // nkv
         hbm = pl.BlockSpec(memory_space=pl.ANY)
-        vmem = pl.BlockSpec(memory_space=pltpu.VMEM)
         dma = pltpu.SemaphoreType.DMA
-        return pl.pallas_call(
+        parts = pl.pallas_call(
             kernel,
-            out_shape=jax.ShapeDtypeStruct((rows, out_w), BF16),
+            out_shape=jax.ShapeDtypeStruct((nkv, rows, out_w), BF16),
             in_specs=[hbm] * 10,
-            out_specs=vmem,
+            out_specs=hbm,
             scratch_shapes=[
                 pltpu.VMEM((nreq, rows, width), BF16),
                 pltpu.VMEM((keys, HD), BF16),
@@ -398,19 +409,19 @@
                 pltpu.VMEM((cols, HD), F32),
                 pltpu.VMEM((nreq, cols), F32),
                 pltpu.VMEM((nkv, rows, out_w), BF16),
-                pltpu.VMEM((nkv, rows, out_w), BF16),
                 dma((10,)),
-                dma((nreq,)),
-                dma((nreq,)),
-                dma((nreq,)),
-                dma((nreq,)),
-                dma((nkv,)),
-                dma((nkv,)),
+                dma,
+                dma((nreq - 1,)),
+                dma,
+                dma((2,)),
+                dma,
+                dma,
             ],
             compiler_params=pltpu.CompilerParams(
                 collective_id=0, has_side_effects=True, vmem_limit_bytes=60 * 2**20
             ),
         )(q, ck, cv, tk, tv, hk, hv, lengths, task_of.reshape(1, -1), w)
+        return jnp.sum(parts.astype(F32), axis=0).astype(BF16)
 
     return jax.shard_map(
         shards,

time: 40.3 us -> 39.1 us (0.970)
  other arithmetic: 0 us -> 1.62 us
  Pallas kernels: 38.7 us -> 37.3 us
  local copies, waits for them, and re-layouts: 1.38 us -> 0 us
    reduce_sum x0 -> x1, other arithmetic: none -> 1.62 us  [shards(): return jnp.sum(parts.astype(F32), axis=0).astype(BF16)]
    pallas_call x1, Pallas kernels: 38.7 us -> 37.3 us  [shards(): pl.pallas_call(kernel, out_shape=jax.ShapeDtypeStruct((nkv, rows, out_w),...]
    unnamed x1 -> x0, local copies, waits for them, and re-layouts: 1.38 us -> none
where the time goes in v4:
time: 39.1 us; the launch traced here: 38.9 us
  Pallas kernels  37.3 us (95%)
  other arithmetic  1.62 us (4%)
    pallas_call x1, Pallas kernels, shards(): pl.pallas_call(kernel, out_shape=jax.ShapeDtypeStruct((nkv, rows, out_w),...  37.3 us
    reduce_sum x1, other arithmetic, shards(): return jnp.sum(parts.astype(F32), axis=0).astype(BF16)  1.62 us

profile of v4, /device:TPU:1, one launch (start us, length us, event | category | flops | bytes accessed | tf_op | source)
XLA Modules:
  0.0 38.9 jit_solution(10425635066658824701)
XLA Ops:
  0.0 37.3 %shard_map.100 = bf16[8,16,1024]{2,1,0:T(8,128)(2,1)} custom-call(bf16[16,1024]{1,0:T(8,128)(2,1)} %q_hbm.1, bf16[4096,128]{1,0:T(8,128)(2,1)} %ck_hbm.1, bf16[4096,128]{1,0:T(8,128)(2,1)} %cv_hbm.1, bf16[2048,128]{1,0:T(8,128)(2,1)} %tk_hbm.1, bf16[2048,128]{1,0:T(8,128)(2,1)} %tv_hbm.1, bf16[8192,128]{1,0:T(8,128)(2,1)} %hk_hbm.1, ...), custom_call_target="tpu_custom_call" | custom-call | tf_op jit(solution)/shard_map/pallas_call | solution.py:387
  37.3 1.6 %reduce_sum.12 = bf16[16,1024]{1,0:T(8,128)(2,1)} reduce(bf16[8,16,1024]{2,1,0:T(8,128)(2,1)} %shard_map.100, bf16[]{:T(256)} %constant.2.clone.1), dimensions={0}, to_apply=%region_0.0 | reduce | flops 114688 | bytes 294914 | tf_op jit(solution)/shard_map/reduce_sum | solution.py:424

commit v5 on v4

--- a/solution.py
+++ b/solution.py
@@ -70,37 +70,38 @@
     nch, ncorp, per = keys // chunk, corpus // chunk, deep // chunk
     me = lax.axis_index("req")
     mj = lax.axis_index("kvh")
-    y, x = me // 4, me % 4
-    mz, mc = mj // 2, mj % 2
-
-    def off(t):
-        dy = 3 - t // 4
-        return dy, (t % 4 + 1 + dy) % 4
-
-    def slot(t):
-        dy, dx = off(t)
-        return dy * 4 + dx
-
-    def peer(t, sign):
-        dy, dx = off(t)
-        return ((y + 4 + sign * dy) % 4) * 4 + (x + 4 + sign * dx) % 4
+    y, x = lax.div(me, 4), lax.rem(me, 4)
+    mz, mc = lax.div(mj, 2), lax.rem(mj, 2)
+
+    def rem4(v):
+        return v % 4 if isinstance(v, int) else lax.rem(v, 4)
+
+    def number(block):
+        return 4 * block[0] + block[1]
+
+    def slot(block):
+        g, a = block
+        return (3 - g) * 4 + rem4(a + 4 - g)
+
+    def source(block):
+        g, a = block
+        return rem4(y + 3 - g) * 4 + rem4(x + a + 4 - g)
+
+    def reader(block):
+        g, a = block
+        return rem4(y + 1 + g) * 4 + rem4(x + 4 - a + g)
+
+    others = [(g, a) for g in range(4) for a in range(4)][:-1]
 
     def greet(**device):
         pl.semaphore_signal(
             pltpu.get_barrier_semaphore(), inc=1, device_id=device, device_id_type=MESH
         )
 
-    def greet_req(t, carry):
-        greet(req=peer(t, -1))
-        return carry
-
-    lax.fori_loop(0, nreq - 1, greet_req, 0)
-
-    def greet_kv(e, carry):
-        greet(kvh=(mj + e) % nkv)
-        return carry
-
-    lax.fori_loop(1, nkv, greet_kv, 0)
+    for block in others:
+        greet(req=reader(block))
+    for e in range(1, nkv):
+        greet(kvh=lax.rem(mj + e, nkv))
 
     loads = [
         pltpu.make_async_copy(q_hbm, q_all.at[0], ld_sem.at[0]),
@@ -120,21 +121,18 @@
     loads[0].wait()
     pl.semaphore_wait(pltpu.get_barrier_semaphore(), nreq + nkv - 2)
 
-    def q_copy(t):
+    def q_copy(block):
         return pltpu.make_async_remote_copy(
             src_ref=q_all.at[0],
-            dst_ref=q_all.at[slot(t)],
+            dst_ref=q_all.at[slot(block)],
             send_sem=q_send,
-            recv_sem=q_recv.at[t],
-            device_id={"req": peer(t, -1)},
+            recv_sem=q_recv.at[number(block)],
+            device_id={"req": reader(block)},
             device_id_type=MESH,
         )
 
-    def send_q(t, carry):
-        q_copy(t).start()
-        return carry
-
-    lax.fori_loop(0, nreq - 1, send_q, 0)
+    for block in others:
+        q_copy(block).start()
 
     def head_major(k):
         block = q_all[k]
@@ -161,12 +159,12 @@
 
     early = nreq - 4
 
-    def arrive(block):
-        for t in block:
-            q_copy(t).wait_recv()
-
-    def q_of(block):
-        return jnp.concatenate([tile for t in block for tile in head_major(slot(t))], 0)
+    def arrive(blocks):
+        for block in blocks:
+            q_copy(block).wait_recv()
+
+    def q_of(blocks):
+        return jnp.concatenate([tile for b in blocks for tile in head_major(slot(b))], 0)
 
     def score(c, q, sref, peaks):
         at = slice(c * chunk, (c + 1) * chunk)
@@ -187,13 +185,14 @@
         part = jnp.dot(vt[:, at], pref[at, :n], preferred_element_type=F32)
         return part if acc is None else acc + part
 
-    def o_copy(t):
+    def o_copy(block):
+        t = number(block)
         return pltpu.make_async_remote_copy(
             src_ref=osend.at[t],
             dst_ref=orecv.at[t],
             send_sem=o_send,
-            recv_sem=o_recv.at[t // early],
-            device_id={"req": peer(t, 1)},
+            recv_sem=o_recv.at[1 if isinstance(t, int) and t >= early else 0],
+            device_id={"req": source(block)},
             device_id_type=MESH,
         )
 
@@ -219,7 +218,7 @@
 
     def stage(now, then, s_now, s_then, pref, peaks):
         n = len(now) * cols
-        mask = jnp.concatenate([valid[pl.ds(peer(t, 1), 1), :] for t in now], 1) > 0
+        mask = jnp.concatenate([valid[pl.ds(source(b), 1), :] for b in now], 1) > 0
         pk = [jnp.max(m, axis=0, keepdims=True) for m in peaks]
         top = jnp.maximum(pk[0], jnp.where(mask, pk[1], -FAR)) * CS
         shifts = [top, jnp.where(mask, top, FAR)]
@@ -241,22 +240,23 @@
         total = acc[HD : HD + 1, :]
         o = (acc[:HD, :] * (1.0 / total)).astype(BF16)
         info = pack(top + jnp.log2(total))
-        for a, t in enumerate(now):
-            at = slice(a * cols, (a + 1) * cols)
+        for i, block in enumerate(now):
+            at = slice(i * cols, (i + 1) * cols)
+            t = number(block)
             osend[t, :HD, :] = o[:, at]
             osend[t, HD:, :] = info[:, at]
             if not isinstance(t, int) or t < nreq - 1:
-                o_copy(t).start()
+                o_copy(block).start()
         return later
 
-    def first_scores(block, sref):
+    def first_scores(blocks, sref):
         peaks = [None, None]
-        q = q_of(block)
+        q = q_of(blocks)
         for c in range(nch):
             score(c, q, sref, peaks)
         return peaks
 
-    stage([nreq - 1], None, sb, None, pb, first_scores([nreq - 1], sb))
+    stage([(3, 3)], None, sb, None, pb, first_scores([(3, 3)], sb))
 
     pr = lax.broadcasted_iota(jnp.int32, (cols, cols), 0)
     pc = lax.broadcasted_iota(jnp.int32, (cols, cols), 1)
@@ -290,18 +290,17 @@
     hot = lax.dot_general(ho, perm16, TN, preferred_element_type=F32)
     hl = jnp.sum(perm * (hm * CS + jnp.log2(htot)), axis=0, keepdims=True)
 
-    arrive([0, 1])
-    peaks = first_scores([0, 1], sa)
-
-    def twice(i, peaks):
-        t = 4 * i
-        peaks = stage([t, t + 1], [t + 2, t + 3], sa, sb, pa, list(peaks))
-        peaks = stage([t + 2, t + 3], [t + 4, t + 5], sb, sa, pb, peaks)
+    arrive([(0, 0), (0, 1)])
+    peaks = first_scores([(0, 0), (0, 1)], sa)
+
+    def twice(g, peaks):
+        peaks = stage([(g, 0), (g, 1)], [(g, 2), (g, 3)], sa, sb, pa, list(peaks))
+        peaks = stage([(g, 2), (g, 3)], [(g + 1, 0), (g + 1, 1)], sb, sa, pb, peaks)
         return tuple(peaks)
 
-    peaks = list(lax.fori_loop(0, nreq // 4 - 1, twice, tuple(peaks)))
-    peaks = stage([nreq - 4, nreq - 3], [nreq - 2], sa, sb, pa, peaks)
-    stage([nreq - 2], None, sb, None, pb, peaks)
+    peaks = list(lax.fori_loop(0, 3, twice, tuple(peaks)))
+    peaks = stage([(3, 0), (3, 1)], [(3, 2)], sa, sb, pa, peaks)
+    stage([(3, 2)], None, sb, None, pb, peaks)
 
     def arrived(t, n):
         pltpu.make_async_remote_copy(
@@ -309,7 +308,7 @@
             dst_ref=orecv.at[pl.ds(t, n)],
             send_sem=o_send,
             recv_sem=o_recv.at[t // early],
-            device_id={"req": peer(0, 1)},
+            device_id={"req": source((0, 0))},
             device_id_type=MESH,
         ).wait_recv()
 
@@ -325,9 +324,12 @@
     loads[9].wait()
 
     def kv_peer(e):
-        dz, dc = e // 2, e % 2
-        dz = dz + dz // 2 - 2 * (dz // 3)
-        return ((mz + dz) % 4) * 2 + (mc + dc) % 2
+        if isinstance(e, int):
+            dz, dc = (0, 1, 3, 2)[e // 2], e % 2
+        else:
+            half, dc = lax.div(e, 2), lax.rem(e, 2)
+            dz = half + lax.div(half, 2) - 2 * lax.div(half, 3)
+        return lax.rem(mz + dz, 4) * 2 + lax.rem(mc + dc, 2)
 
     def p_copy(e):
         return pltpu.make_async_remote_copy(
@@ -364,9 +366,9 @@
             device_id_type=MESH,
         )
 
-    others = pl.ds(1, nreq - 1)
-    whole(q_all.at[others], q_all.at[others], q_send, q_recv.at[0]).wait_send()
-    whole(osend.at[others], orecv.at[others], o_send, o_recv.at[0]).wait_send()
+    most = pl.ds(0, nreq - 1)
+    whole(q_all.at[most], q_all.at[most], q_send, q_recv.at[0]).wait_send()
+    whole(osend.at[most], orecv.at[most], o_send, o_recv.at[0]).wait_send()
     parts = whole(psend.at[pl.ds(1, nkv - 1)], out_ref.at[pl.ds(1, nkv - 1)], p_send, p_recv)
     parts.wait_send()
     parts.wait_recv()

time: 39.1 us -> 38.9 us (level)
  no operation moved by 1% of the time
where the time goes in v5:
time: 38.9 us; the launch traced here: 38.8 us
  Pallas kernels  37.1 us (95%)
  other arithmetic  1.62 us (4%)
    pallas_call x1, Pallas kernels, shards(): pl.pallas_call(kernel, out_shape=jax.ShapeDtypeStruct((nkv, rows, out_w),...  37.1 us
    reduce_sum x1, other arithmetic, shards(): return jnp.sum(parts.astype(F32), axis=0).astype(BF16)  1.62 us

profile of v5, /device:TPU:1, one launch (start us, length us, event | category | flops | bytes accessed | tf_op | source)
XLA Modules:
  0.0 38.8 jit_solution(15261525010615834717)
XLA Ops:
  0.0 37.1 %shard_map.100 = bf16[8,16,1024]{2,1,0:T(8,128)(2,1)} custom-call(bf16[16,1024]{1,0:T(8,128)(2,1)} %q_hbm.1, bf16[4096,128]{1,0:T(8,128)(2,1)} %ck_hbm.1, bf16[4096,128]{1,0:T(8,128)(2,1)} %cv_hbm.1, bf16[2048,128]{1,0:T(8,128)(2,1)} %tk_hbm.1, bf16[2048,128]{1,0:T(8,128)(2,1)} %tv_hbm.1, bf16[8192,128]{1,0:T(8,128)(2,1)} %hk_hbm.1, ...), custom_call_target="tpu_custom_call" | custom-call | tf_op jit(solution)/shard_map/pallas_call | solution.py:389
  37.1 1.6 %reduce_sum.12 = bf16[16,1024]{1,0:T(8,128)(2,1)} reduce(bf16[8,16,1024]{2,1,0:T(8,128)(2,1)} %shard_map.100, bf16[]{:T(256)} %constant.2.clone.1), dimensions={0}, to_apply=%region_0.0 | reduce | flops 114688 | bytes 294914 | tf_op jit(solution)/shard_map/reduce_sum | solution.py:426

commit v6 on v5

--- a/solution.py
+++ b/solution.py
@@ -149,8 +149,9 @@
     valid[...] = jnp.dot(mine, spread, preferred_element_type=F32)
 
     loads[3].wait()
-    loads[4].wait()
     for c in range(nch):
+        if c == ncorp:
+            loads[4].wait()
         at = slice(c * chunk, (c + 1) * chunk)
         vt[:HD, at] = vbuf[at, :].T
     vt[HD:, :] = jnp.ones((vt.shape[0] - HD, keys), BF16)
@@ -216,7 +217,13 @@
         o = functools.reduce(jnp.add, [o * (w * inv) for (o, _), w in zip(parts, ws)])
         return o, top + jnp.log2(den)
 
-    def stage(now, then, s_now, s_then, pref, peaks):
+    def go_home(blocks):
+        for block in blocks:
+            t = number(block)
+            if not isinstance(t, int) or t < nreq - 1:
+                o_copy(block).start()
+
+    def stage(now, then, s_now, s_then, pref, peaks, alone=True):
         n = len(now) * cols
         mask = jnp.concatenate([valid[pl.ds(source(b), 1), :] for b in now], 1) > 0
         pk = [jnp.max(m, axis=0, keepdims=True) for m in peaks]
@@ -224,7 +231,8 @@
         shifts = [top, jnp.where(mask, top, FAR)]
         later = [None, None]
         if then:
-            arrive(then)
+            if alone:
+                arrive(then)
             q = q_of(then)
         acc, done = None, 0
         for c in range(nch):
@@ -245,8 +253,8 @@
             t = number(block)
             osend[t, :HD, :] = o[:, at]
             osend[t, HD:, :] = info[:, at]
-            if not isinstance(t, int) or t < nreq - 1:
-                o_copy(block).start()
+        if alone:
+            go_home(now)
         return later
 
     def first_scores(blocks, sref):
@@ -294,8 +302,13 @@
     peaks = first_scores([(0, 0), (0, 1)], sa)
 
     def twice(g, peaks):
-        peaks = stage([(g, 0), (g, 1)], [(g, 2), (g, 3)], sa, sb, pa, list(peaks))
-        peaks = stage([(g, 2), (g, 3)], [(g + 1, 0), (g + 1, 1)], sb, sa, pb, peaks)
+        one, two = [(g, 0), (g, 1)], [(g, 2), (g, 3)]
+        three = [(g + 1, 0), (g + 1, 1)]
+        arrive(two)
+        peaks = stage(one, two, sa, sb, pa, list(peaks), alone=False)
+        arrive(three)
+        peaks = stage(two, three, sb, sa, pb, peaks, alone=False)
+        go_home(one + two)
         return tuple(peaks)
 
     peaks = list(lax.fori_loop(0, 3, twice, tuple(peaks)))

time: 38.9 us -> 38.9 us (level)
  no operation moved by 1% of the time
where the time goes in v6:
time: 38.9 us; the launch traced here: 38.8 us
  Pallas kernels  37.1 us (95%)
  other arithmetic  1.62 us (4%)
    pallas_call x1, Pallas kernels, shards(): pl.pallas_call(kernel, out_shape=jax.ShapeDtypeStruct((nkv, rows, out_w),...  37.1 us
    reduce_sum x1, other arithmetic, shards(): return jnp.sum(parts.astype(F32), axis=0).astype(BF16)  1.62 us

profile of v6, /device:TPU:1, one launch (start us, length us, event | category | flops | bytes accessed | tf_op | source)
XLA Modules:
  0.0 38.8 jit_solution(311133157124534808)
XLA Ops:
  0.0 37.1 %shard_map.100 = bf16[8,16,1024]{2,1,0:T(8,128)(2,1)} custom-call(bf16[16,1024]{1,0:T(8,128)(2,1)} %q_hbm.1, bf16[4096,128]{1,0:T(8,128)(2,1)} %ck_hbm.1, bf16[4096,128]{1,0:T(8,128)(2,1)} %cv_hbm.1, bf16[2048,128]{1,0:T(8,128)(2,1)} %tk_hbm.1, bf16[2048,128]{1,0:T(8,128)(2,1)} %tv_hbm.1, bf16[8192,128]{1,0:T(8,128)(2,1)} %hk_hbm.1, ...), custom_call_target="tpu_custom_call" | custom-call | tf_op jit(solution)/shard_map/pallas_call | solution.py:402
  37.1 1.6 %reduce_sum.12 = bf16[16,1024]{1,0:T(8,128)(2,1)} reduce(bf16[8,16,1024]{2,1,0:T(8,128)(2,1)} %shard_map.100, bf16[]{:T(256)} %constant.2.clone.1), dimensions={0}, to_apply=%region_0.0 | reduce | flops 114688 | bytes 294914 | tf_op jit(solution)/shard_map/reduce_sum | solution.py:439
